TPU v7x, 512 devices: a whole 4x4x16 slice. The times are simulated.
512 devices in a mesh: seq: 32 (over x_hi, z), lat: 16 (over x_lo, y, core).
Axes of the slice: x: 4 (x_hi: 2, x_lo: 2; x = x_hi * 2 + x_lo), y: 4, z: 16, core: 2. Of those that a mesh axis runs over, the one named last changes fastest.
Arguments:
- inputs: bfloat16 [24576, 2048], P('seq'), may hold values from -6 to 6
- cross_kv: bfloat16 [2048, 2, 2048], P(None, None, 'lat'), may hold values from -0.125 to 0.125
- cross_out_w: bfloat16 [2048, 2048], P('lat'), may hold values from -0.5 to 0.5
- latent_query: bfloat16 [1024, 2048], P('seq', 'lat')
- latent_base: bfloat16 [1024, 2048], P('seq'), may hold values from -1.75 to 1.75
- latent_pos: int32 [1024], replicated, may hold values from 0 to 24575, as said below
- attn_qkv: bfloat16 [1, 2048, 3, 2048], P(None, 'seq', None, 'lat'), may hold values from -0.125 to 0.125
- attn_out: bfloat16 [1, 2048, 2048], P(None, 'seq', 'lat'), may hold values from -2 to 2
- mlp_up: bfloat16 [1, 2048, 8192], P(None, 'seq', 'lat'), may hold values from -0.125 to 0.125
- mlp_down: bfloat16 [1, 2048, 8192], P(None, 'seq', 'lat'), may hold values from -0.0625 to 0.0625
Outputs:
- latent_out: bfloat16 [1024, 2048], P(('seq', 'lat'))
Inputs may be any that keep to these rules, and one draw needn't show every extreme that they name: `latent_pos`: strictly increasing along the latents; the last latent sits at position 24575.
All inputs are finite; a program needn't handle non-finite values.
Results may differ from a plain program's by a relative error of at most 0.025.
Values may be sent and summed in bfloat16 or wider, within the bound.
A program may use at most 64 MiB of HBM per device.

v0:
```python
import math

import jax
import jax.numpy as jnp
from jax import lax
from jax.sharding import PartitionSpec as P

HD = 128
LAT_DEV = 32


def combined_all(part, axis, combine):
    gathered = jax.tree.map(lambda a: lax.all_gather(a, axis), part)

    def take(source):
        return jax.tree.map(lambda a: lax.dynamic_index_in_dim(a, source, 0, False), gathered)

    return lax.fori_loop(
        1, lax.axis_size(axis), lambda source, state: combine(state, take(source)), take(0)
    )


def rms(h):
    return h * lax.rsqrt(jnp.mean(h * h, axis=-1, keepdims=True) + 1e-06)


def combine(first, second):
    top = jnp.maximum(first[0], second[0])
    left = jnp.exp(first[0] - top)
    right = jnp.exp(second[0] - top)
    return (
        top,
        first[1] * left + second[1] * right,
        first[2] * left[:, None] + second[2] * right[:, None],
    )


def add_heads(h, term):
    return h + lax.psum(term, "lat")


def normed_rows(h):
    normed = rms(h).astype(jnp.bfloat16)
    return normed


def local(
    inputs,
    cross_kv,
    cross_out_w,
    latent_query,
    latent_base,
    latent_pos,
    attn_qkv,
    attn_out,
    mlp_up,
    mlp_down,
):
    scale = 1.0 / math.sqrt(HD)
    seq_index = lax.axis_index("seq")
    lat_index = lax.axis_index("lat")
    tok_rows = inputs.shape[0]
    share = LAT_DEV // lax.axis_size("lat")
    queries, qkv_w, out_w, up_w, down_w = (
        lax.all_gather(latent_query, "seq", axis=0, tiled=True),
        lax.all_gather(attn_qkv, "seq", axis=1, tiled=True),
        lax.all_gather(attn_out, "seq", axis=1, tiled=True),
        lax.all_gather(mlp_up, "seq", axis=1, tiled=True),
        lax.all_gather(mlp_down, "seq", axis=1, tiled=True),
    )
    keyvals = jnp.einsum(
        "td,dch->tch", inputs, cross_kv, preferred_element_type=jnp.float32
    ).astype(jnp.bfloat16)
    key_pos = seq_index * tok_rows + jnp.arange(tok_rows, dtype=jnp.int32)
    allowed = key_pos[None, :] <= latent_pos[:, None]
    scores = (
        jnp.einsum("lh,th->lt", queries, keyvals[:, 0], preferred_element_type=jnp.float32) * scale
    )
    local_top = jnp.max(jnp.where(allowed, scores, -1e30), axis=1)
    weights = jnp.where(allowed, jnp.exp(scores - local_top[:, None]), 0.0)
    local_total = jnp.sum(weights, axis=1)
    local_numer = jnp.dot(
        weights.astype(jnp.bfloat16), keyvals[:, 1], preferred_element_type=jnp.float32
    )
    first_row = seq_index * LAT_DEV
    top, total, numer = combined_all((local_top, local_total, local_numer), "seq", combine)
    total = lax.dynamic_slice_in_dim(total, first_row, LAT_DEV)
    numer = lax.dynamic_slice_in_dim(numer, first_row, LAT_DEV)
    context = (numer / total[:, None]).astype(jnp.bfloat16)
    h = latent_base.astype(jnp.float32)
    h = add_heads(h, jnp.dot(context, cross_out_w, preferred_element_type=jnp.float32))
    my_rows = first_row + jnp.arange(LAT_DEV, dtype=jnp.int32)
    normed = normed_rows(h)
    qkv = jnp.einsum("ld,dch->lch", normed, qkv_w[0], preferred_element_type=jnp.float32).astype(
        jnp.bfloat16
    )
    query = qkv[:, 0]
    piece = lax.all_gather(qkv[:, 1:], "seq", axis=0, tiled=True)
    raw = jnp.einsum("lh,th->lt", query, piece[:, 0], preferred_element_type=jnp.float32) * scale
    capped = 30.0 * jnp.tanh(raw / 30.0)
    key_rows = jnp.arange(piece.shape[0], dtype=jnp.int32)
    expo = jnp.where(key_rows[None, :] <= my_rows[:, None], jnp.exp(capped), 0.0)
    self_total = jnp.sum(expo, axis=1)
    self_numer = jnp.dot(expo.astype(jnp.bfloat16), piece[:, 1], preferred_element_type=jnp.float32)
    self_context = (self_numer / self_total[:, None]).astype(jnp.bfloat16)
    h = add_heads(
        h, jnp.einsum("lh,dh->ld", self_context, out_w[0], preferred_element_type=jnp.float32)
    )
    normed2 = normed_rows(h)
    hidden = jax.nn.gelu(jnp.dot(normed2, up_w[0], preferred_element_type=jnp.float32)).astype(
        jnp.bfloat16
    )
    h = add_heads(h, jnp.einsum("lf,df->ld", hidden, down_w[0], preferred_element_type=jnp.float32))
    h = lax.dynamic_slice_in_dim(h, lat_index * share, share)
    return h.astype(jnp.bfloat16)


def solution(mesh):
    return jax.shard_map(
        local,
        mesh=mesh,
        in_specs=(
            P("seq", None),
            P(None, None, "lat"),
            P("lat", None),
            P("seq", "lat"),
            P("seq", None),
            P(),
            P(None, "seq", None, "lat"),
            P(None, "seq", "lat"),
            P(None, "seq", "lat"),
            P(None, "seq", "lat"),
        ),
        out_specs=P(("seq", "lat"), None),
        check_vma=False,
    )
```

profile of v0, /device:TPU:1, one launch (start us, length us, event | category | flops | bytes accessed | tf_op | source)
XLA Modules:
  0.0 1381.0 jit_solution(1255034608973008092)
XLA Ops:
  6.5 71.1 %all_gather.36 = bf16[1024,128]{1,0:T(8,128)(2,1)S(1)} all-gather(bf16[32,128]{1,0:T(8,128)(2,1)} %param.15), channel_id=1, replica_groups=mesh['seq'=32,'lat'=16] {'seq'}, dimensions={0}, use_global_device_ids=true | all-gather | bytes 270336 | tf_op jit(solution)/shard_map/all_gather | solution.py:65
  83.9 2.6 fusion.6
  86.5 57.5 %all-gather.1 = f32[32768]{0:T(1024)S(1)} all-gather(f32[1024]{0:T(1024)S(1)} %fusion.6), channel_id=3, replica_groups=mesh['seq'=32,'lat'=16] {'seq'}, dimensions={0}, use_global_device_ids=true | all-gather | bytes 135168 | tf_op jit(solution)/shard_map/all_gather | solution.py:13
  144.0 60.5 %all-gather = f32[32768]{0:T(1024)S(1)} all-gather(f32[1024]{0:T(1024)S(1)} %get-tuple-element.206), channel_id=2, replica_groups=mesh['seq'=32,'lat'=16] {'seq'}, dimensions={0}, use_global_device_ids=true | all-gather | bytes 135168 | tf_op jit(solution)/shard_map/all_gather | solution.py:13
  205.2 150.6 %all-gather.14.cloned.1.call-done = f32[32768,128]{1,0:T(8,128)} async-done(((f32[1024,128]{1,0:T(8,128)}), f32[32768,128]{1,0:T(8,128)}) %all-gather.14.cloned.1.call-update) | async-done | bytes 16777232 | tf_op jit(solution)/shard_map/all_gather | solution.py:13
  357.6 96.9 %while.19 = (s32[]{:T(128)}, f32[1024]{0:T(1024)S(1)}, f32[1024]{0:T(1024)S(1)}, f32[1024,128]{1,0:T(8,128)}, f32[32,1024]{1,0:T(8,128)}, /*index=5*/f32[32,1024...) while((s32[]{:T(128)}, f32[1024]{0:T(1024)S(1)}, f32[1024]{0:T(1024)S(1)}, ...), condition=%wide.region_3.4_spmd, body=%wide.region_2.3_spmd.sunk | while | flops 399365 | bytes 1630359 | solution.py:18
  358.4 2.3 fusion.73
  361.6 2.3 fusion.73
  377.2 2.3 fusion.73
  380.3 2.3 fusion.73
  383.4 2.3 fusion.73
  395.9 2.3 fusion.73
  399.1 2.3 fusion.73
  402.2 2.3 fusion.73
  414.7 2.3 fusion.73
  457.5 64.6 %all_gather.45 = bf16[1,2048,128]{2,1,0:T(8,128)(2,1)} all-gather(bf16[1,64,128]{2,1,0:T(8,128)(2,1)S(1)} %copy-done.5), channel_id=1, replica_groups=mesh['seq'=32,'lat'=16] {'seq'}, dimensions={1}, use_global_device_ids=true | all-gather | bytes 540672 | tf_op jit(solution)/shard_map/all_gather | solution.py:67
  522.0 62.4 %all-reduce.4.cloned.1.call-done = f32[32,2048]{1,0:T(8,128)} async-done(((f32[32,2048]{1,0:T(8,128)}), f32[32,2048]{1,0:T(8,128)}) %all-reduce.4.cloned.1.call-update) | async-done | bytes 262160 | tf_op jit(solution)/shard_map/psum | solution.py:39
  585.6 141.4 %all-gather.8.cloned.1.call-done = bf16[1,2048,3,128]{3,1,2,0:T(8,128)(2,1)} async-done(((bf16[1,64,3,128]{3,1,2,0:T(8,128)(2,1)}), bf16[1,2048,3,128]{3,1,2,0:T(8,128)(2,1)}) %all-gather.8.cloned.1.call-update) | async-done | bytes 1572880 | tf_op jit(solution)/shard_map/all_gather | solution.py:66
  728.9 61.3 %all_gather.44 = bf16[1024,2,128]{2,0,1:T(8,128)(2,1)S(1)} all-gather(bf16[32,2,128]{2,0,1:T(8,128)(2,1)S(1)} %slice.36), channel_id=1, replica_groups=mesh['seq'=32,'lat'=16] {'seq'}, dimensions={0}, use_global_device_ids=true | all-gather | bytes 540672 | tf_op jit(solution)/shard_map/all_gather | solution.py:98
  795.5 144.6 %all-reduce.6.cloned.1.call-done = f32[32,2048]{1,0:T(8,128)} async-done(((f32[32,2048]{1,0:T(8,128)}), f32[32,2048]{1,0:T(8,128)}) %all-reduce.6.cloned.1.call-update) | async-done | bytes 262160 | tf_op jit(solution)/shard_map/psum | solution.py:39
  942.0 143.5 %all-gather.10.cloned.1.call-done = bf16[1,2048,512]{2,1,0:T(8,128)(2,1)} async-done(((bf16[1,64,512]{2,1,0:T(8,128)(2,1)}), bf16[1,2048,512]{2,1,0:T(8,128)(2,1)}) %all-gather.10.cloned.1.call-update) | async-done | bytes 2097168 | tf_op jit(solution)/shard_map/all_gather | solution.py:68
  1085.5 147.6 %all-gather.12.cloned.1.call-done = bf16[1,2048,512]{2,1,0:T(8,128)(2,1)} async-done(((bf16[1,64,512]{2,1,0:T(8,128)(2,1)}), bf16[1,2048,512]{2,1,0:T(8,128)(2,1)}) %all-gather.12.cloned.1.call-update) | async-done | bytes 2097168 | tf_op jit(solution)/shard_map/all_gather | solution.py:69
  1233.0 4.2 fusion.7
  1237.3 135.4 %all-reduce.8.cloned.1.call-done = f32[32,2048]{1,0:T(8,128)} async-done(((f32[32,2048]{1,0:T(8,128)}), f32[32,2048]{1,0:T(8,128)}) %all-reduce.8.cloned.1.call-update) | async-done | bytes 262160 | tf_op jit(solution)/shard_map/psum | solution.py:39
  (133 shorter events, 99.1 us)
Async XLA Ops:
  6.5 71.1 %copy-start = (bf16[768,2048]{1,0:T(8,128)(2,1)S(1)}, bf16[768,2048]{1,0:T(8,128)(2,1)}, u32[]{:S(2)}) copy-start(bf16[768,2048]{1,0:T(8,128)(2,1)} %param.12) | copy-start | bytes 9437188
  6.5 349.2 %all-gather.14.cloned.1.call-start = ((), (), s32[]{:S(2)}) async-start(), calls=%async_computation.6 | async-start | bytes 17301504 | tf_op jit(solution)/shard_map/all_gather | solution.py:13
  77.6 2.2 copy-start.6
  80.5 1.6 copy-start.1
  83.9 500.6 %all-reduce.4.cloned.1.call-start = ((), (), s32[]{:S(2)}) async-start(), calls=%async_computation | async-start | bytes 524288 | tf_op jit(solution)/shard_map/psum | solution.py:39
  357.6 99.8 %copy-start.5 = (bf16[1,64,128]{2,1,0:T(8,128)(2,1)S(1)}, bf16[1,64,128]{2,1,0:T(8,128)(2,1)}, u32[]{:S(2)}) copy-start(bf16[1,64,128]{2,1,0:T(8,128)(2,1)} %param.19) | copy-start | bytes 49156
  357.6 226.8 %copy-start.3 = (bf16[32,2048]{1,0:T(8,128)(2,1)S(1)}, bf16[32,2048]{1,0:T(8,128)(2,1)}, u32[]{:S(2)}) copy-start(bf16[32,2048]{1,0:T(8,128)(2,1)} %param.16) | copy-start | bytes 393220
  456.7 270.3 %all-gather.8.cloned.1.call-start = ((), (), s32[]{:S(2)}) async-start(), calls=%async_computation.1 | async-start | bytes 1622016 | tf_op jit(solution)/shard_map/all_gather | solution.py:66
  457.4 482.7 %all-reduce.6.cloned.1.call-start = ((), (), s32[]{:S(2)}) async-start(), calls=%async_computation.2 | async-start | bytes 524288 | tf_op jit(solution)/shard_map/psum | solution.py:39
  584.5 355.7 %copy-start.2 = (f32[32,2048]{1,0:T(8,128)S(1)}, f32[32,2048]{1,0:T(8,128)}, u32[]{:S(2)}) copy-start(f32[32,2048]{1,0:T(8,128)} %all-reduce.4.cloned.1.call-done) | copy-start | bytes 786436
  790.2 0.8 copy-start.4
  794.3 291.2 %all-gather.10.cloned.1.call-start = ((), (), s32[]{:S(2)}) async-start(), calls=%async_computation.3 | async-start | bytes 2162688 | tf_op jit(solution)/shard_map/all_gather | solution.py:68
  794.9 438.2 %all-gather.12.cloned.1.call-start = ((), (), s32[]{:S(2)}) async-start(), calls=%async_computation.4 | async-start | bytes 2162688 | tf_op jit(solution)/shard_map/all_gather | solution.py:69
  795.5 577.2 %all-reduce.8.cloned.1.call-start = ((), (), s32[]{:S(2)}) async-start(), calls=%async_computation.5 | async-start | bytes 524288 | tf_op jit(solution)/shard_map/psum | solution.py:39
Sparse Core Ops, SparseCore 0:
  84.0 271.7 all-gather.13
  456.8 127.6 all-reduce.3
  588.0 138.9 all-gather.7
  794.4 145.6 all-reduce.5
  943.1 142.3 all-gather.9
  1088.4 144.5 all-gather.11
  1237.4 135.2 all-reduce.7
where the time goes:
time: 1380 us
  waiting for transfers between devices  927 us (67%)
  blocking collectives  315 us (23%)
  other arithmetic  80.2 us (6%)
  local copies, waits for them, and re-layouts  28.9 us (2%)
  matrix products  15.9 us (1%)
    psum x3, waiting for transfers between devices, add_heads(): return h + lax.psum(term, 'lat')  342 us
    all_gather x1, waiting for transfers between devices, combined_all(): gathered = jax.tree.map(lambda a: lax.all_gather(a, axis), part)  151 us
    all_gather x1, waiting for transfers between devices, local(): lax.all_gather(mlp_down, 'seq', axis=1, tiled=True)  148 us
    all_gather x1, waiting for transfers between devices, local(): lax.all_gather(mlp_up, 'seq', axis=1, tiled=True)  144 us
    all_gather x1, waiting for transfers between devices, local(): lax.all_gather(attn_qkv, 'seq', axis=1, tiled=True)  141 us
    all_gather x2, blocking collectives, combined_all(): gathered = jax.tree.map(lambda a: lax.all_gather(a, axis), part)  118 us
    add x31, other arithmetic, combine(): first[2] * left[:, None] + second[2] * right[:, None]  72.7 us
    all_gather x1, blocking collectives, local(): lax.all_gather(latent_query, 'seq', axis=0, tiled=True)  71.1 us
  transfers between devices with their start and end apart: 7, of which 7 were waited for; matrix products, arithmetic and copies ran while one was open for 0% of the time, Pallas kernels for 0%

commit v1 on v0

v1 whole, which is shorter than its diff:
```python
import math

import jax
import jax.numpy as jnp
from jax import lax
from jax.experimental import pallas as pl
from jax.experimental.pallas import tpu as pltpu
from jax.sharding import PartitionSpec as P

HD = 128
NSEQ = 32
NZ = 16
NLAT = 16
ROWS = 32
LATENTS = 1024
TOK = 768
D = 2048
HID = 512
CHUNK = 64
MESH = pl.DeviceIdType.MESH
F32 = jnp.float32
BF16 = jnp.bfloat16
LOG2E = 1.4426950408889634
SCALE = 1.0 / math.sqrt(HD)
LOW = -1e30


def dot_nt(a, b):
    return lax.dot_general(a, b, (((1,), (1,)), ((), ())), preferred_element_type=F32)


def dot_nn(a, b):
    return jnp.dot(a, b, preferred_element_type=F32)


def kernel(
    x_hbm,
    ckv_hbm,
    wo_ref,
    q_ref,
    base_ref,
    pos_ref,
    w0_ref,
    w1_ref,
    w2_ref,
    out_ref,
    xv,
    ckvv,
    keys,
    vals,
    qbuf,
    wbuf,
    csend,
    crecv,
    lsend,
    lrecv,
    lmat,
    ltr,
    rsend,
    rrecv,
    hsend,
    gath,
    kvbuf,
    part,
    fsend,
    frecv,
    load_sem,
    qs_sem,
    qr_sem,
    ws_sem,
    wf_sem,
    wb_sem,
    wx_sem,
    cs_sem,
    cr_sem,
    ls_sem,
    lr_sem,
    rs_sem,
    rr_sem,
    gs_sem,
    gr_sem,
    ks_sem,
    kr_sem,
    fs_sem,
    fr_sem,
):
    me = lax.axis_index("seq")
    lme = lax.axis_index("lat")
    xh = me // NZ
    z = lax.rem(me, NZ)
    partner = lax.rem(me + NZ, NSEQ)
    z_up = xh * NZ + lax.rem(z + 1, NZ)
    z_down = xh * NZ + lax.rem(z + NZ - 1, NZ)
    my_quad = me // 4

    load_x = pltpu.make_async_copy(x_hbm, xv, load_sem.at[0])
    load_kv = pltpu.make_async_copy(ckv_hbm, ckvv, load_sem.at[1])
    load_x.start()
    load_kv.start()

    kvbuf[...] = jnp.zeros_like(kvbuf)

    barrier = pltpu.get_barrier_semaphore()

    def greet_seq(i, carry):
        pl.semaphore_signal(
            barrier,
            inc=1,
            device_id={"seq": lax.rem(me + i, NSEQ)},
            device_id_type=MESH,
        )
        return carry

    def greet_lat(i, carry):
        pl.semaphore_signal(
            barrier,
            inc=1,
            device_id={"lat": lax.rem(lme + i, NLAT)},
            device_id_type=MESH,
        )
        return carry

    lax.fori_loop(1, NSEQ, greet_seq, 0)
    lax.fori_loop(1, NLAT, greet_lat, 0)

    qbuf[me] = q_ref[...]
    wbuf[0, me] = w0_ref[...]
    wbuf[1, me] = w1_ref[...]
    wbuf[2, me] = w2_ref[...]

    pl.semaphore_wait(barrier, NSEQ - 1 + NLAT - 1)

    def drain(ref, sem):
        pltpu.make_async_copy(ref, ref, sem).wait()

    def send_query(i, carry):
        p = lax.rem(me + i, NSEQ)
        pltpu.make_async_remote_copy(
            src_ref=qbuf.at[me],
            dst_ref=qbuf.at[me],
            send_sem=qs_sem,
            recv_sem=qr_sem.at[my_quad],
            device_id={"seq": p},
            device_id_type=MESH,
        ).start()
        return carry

    lax.fori_loop(1, NSEQ, send_query, 0)

    def move(r, src, to, recv_sem):
        return pltpu.make_async_remote_copy(
            src_ref=wbuf.at[r, src],
            dst_ref=wbuf.at[r, src],
            send_sem=ws_sem.at[r],
            recv_sem=recv_sem,
            device_id={"seq": to},
            device_id_type=MESH,
        )

    def from_below(k):
        return xh * NZ + lax.rem(z + NZ - k, NZ)

    def from_above(k):
        return xh * NZ + lax.rem(z + k, NZ)

    def ring_start(r):
        move(r, me, z_up, wf_sem.at[r, 1]).start()
        move(r, me, z_down, wb_sem.at[r, 1]).start()
        move(r, me, partner, wx_sem.at[r]).start()

    def ring_step(r, k):
        low = from_below(k)
        move(r, low, z_up, wf_sem.at[r, k]).wait_recv()

        @pl.when(k < 8)
        def _():
            move(r, low, z_up, wf_sem.at[r, k + 1]).start()

        move(r, low, partner, wx_sem.at[r]).start()

        @pl.when(k < 8)
        def _():
            high = from_above(k)
            move(r, high, z_down, wb_sem.at[r, k]).wait_recv()

            @pl.when(k < 7)
            def _():
                move(r, high, z_down, wb_sem.at[r, k + 1]).start()

            move(r, high, partner, wx_sem.at[r]).start()

    def ring_steps(r, first, last):
        def body(k, carry):
            ring_step(r, k)
            return carry

        lax.fori_loop(first, last + 1, body, 0)

    def ring_finish(r):
        other = (1 - xh) * NZ
        drain(wbuf.at[r, pl.ds(other, NZ)], wx_sem.at[r])

    def ring_sent(r):
        drain(wbuf.at[r, pl.ds(0, 31)], ws_sem.at[r])

    ring_start(0)

    load_kv.wait()
    load_x.wait()
    for half in range(2):
        rows = pl.ds(half * (TOK // 2), TOK // 2)
        kv = dot_nn(xv[rows, :], ckvv[...])
        keys[rows, :] = kv[:, :HD].astype(BF16)
        vals[rows, :] = kv[:, HD:].astype(BF16)

    key_pos = me * TOK + lax.broadcasted_iota(jnp.int32, (1, TOK), 1)

    def quad_step(j, carry):
        quad = lax.rem(my_quad + j, 8)

        @pl.when(j == 0)
        def _():
            drain(qbuf.at[pl.ds(0, 3)], qr_sem.at[quad])

        @pl.when(j > 0)
        def _():
            drain(qbuf.at[pl.ds(0, 4)], qr_sem.at[quad])

        q = qbuf[pl.ds(quad * 4, 4)].reshape(4 * ROWS, HD)
        scores = dot_nt(q, keys[...])
        pos = pos_ref[pl.ds(pl.multiple_of(quad * 128, 128), 128), :]
        allowed = key_pos <= pos
        top = jnp.max(jnp.where(allowed, scores, LOW), axis=1, keepdims=True)
        weights = jnp.where(allowed, jnp.exp2((scores - top) * (SCALE * LOG2E)), 0.0)
        total = jnp.sum(weights, axis=1, keepdims=True)
        numer = dot_nn(weights.astype(BF16), vals[...])
        some = total > 0.0
        ctx = numer / jnp.where(some, total, 1.0)
        lse = jnp.where(some, top * (SCALE * LOG2E) + jnp.log2(jnp.where(some, total, 1.0)), LOW)
        csend[pl.ds(quad * 4, 4)] = ctx.astype(BF16).reshape(4, ROWS, HD)
        lsend[quad] = jnp.broadcast_to(lse, (128, 128)).T[0:1, :]

        def send_part(t, carry):
            p = quad * 4 + t

            @pl.when(p != me)
            def _():
                pltpu.make_async_remote_copy(
                    src_ref=csend.at[p],
                    dst_ref=crecv.at[me],
                    send_sem=cs_sem,
                    recv_sem=cr_sem,
                    device_id={"seq": p},
                    device_id_type=MESH,
                ).start()
                pltpu.make_async_remote_copy(
                    src_ref=lsend.at[quad],
                    dst_ref=lrecv.at[me],
                    send_sem=ls_sem,
                    recv_sem=lr_sem,
                    device_id={"seq": p},
                    device_id_type=MESH,
                ).start()

            return carry

        lax.fori_loop(0, 4, send_part, 0)
        ring_step(0, j + 1)
        return carry

    lax.fori_loop(0, 8, quad_step, 0)

    crecv[me] = csend[me]
    lrecv[me] = lsend[my_quad]
    ring_start(1)
    drain(qbuf.at[pl.ds(0, 31)], qs_sem)
    ring_steps(1, 1, 4)
    drain(crecv.at[pl.ds(0, 31)], cr_sem)
    drain(lrecv.at[pl.ds(0, 31)], lr_sem)

    for s in range(NSEQ):
        lmat[s : s + 1, :] = lrecv[s]
    logs = lmat[0:NSEQ, :]
    share = jnp.exp2(logs - jnp.max(logs, axis=0, keepdims=True))
    lmat[0:NSEQ, :] = share / jnp.sum(share, axis=0, keepdims=True)
    lmat[NSEQ:, :] = jnp.zeros((128 - NSEQ, 128), F32)
    ltr[...] = lmat[...].T
    mine = ltr[pl.ds(pl.multiple_of(lax.rem(me, 4) * ROWS, ROWS), ROWS), :]
    context = jnp.zeros((ROWS, HD), F32)
    for s in range(NSEQ):
        context += mine[:, s : s + 1] * crecv[s].astype(F32)

    def scatter_start(n, term):
        for f in range(NLAT):
            rsend[n, f] = term[:, f * HD : (f + 1) * HD].astype(BF16)

        def send(i, carry):
            p = lax.rem(lme + i, NLAT)
            pltpu.make_async_remote_copy(
                src_ref=rsend.at[n, p],
                dst_ref=rrecv.at[n, i],
                send_sem=rs_sem.at[n],
                recv_sem=rr_sem.at[n],
                device_id={"lat": p},
                device_id_type=MESH,
            ).start()
            return carry

        lax.fori_loop(1, NLAT, send, 0)

    def scatter_finish(n):
        drain(rrecv.at[n, pl.ds(1, NLAT - 1)], rr_sem.at[n])
        acc = rsend[n, lme].astype(F32)
        for i in range(1, NLAT):
            acc += rrecv[n, i].astype(F32)
        return acc

    def gather_start(n, h):
        hsend[n] = h.astype(BF16)
        gath[n, lme] = h.astype(BF16)

        def send(i, carry):
            pltpu.make_async_remote_copy(
                src_ref=hsend.at[n],
                dst_ref=gath.at[n, lme],
                send_sem=gs_sem.at[n],
                recv_sem=gr_sem.at[n],
                device_id={"lat": lax.rem(lme + i, NLAT)},
                device_id_type=MESH,
            ).start()
            return carry

        lax.fori_loop(1, NLAT, send, 0)

    def gather_finish(n):
        drain(gath.at[n, pl.ds(0, NLAT - 1)], gr_sem.at[n])
        rows = jnp.concatenate([gath[n, f] for f in range(NLAT)], axis=1)
        wide = rows.astype(F32)
        gain = lax.rsqrt(jnp.mean(wide * wide, axis=-1, keepdims=True) + 1e-06)
        return rows, gain

    def weight(r):
        return wbuf[r].reshape(D, HID)

    my_cols = pl.ds(pl.multiple_of(lme * HD, HD), HD)
    scatter_start(0, dot_nn(context.astype(BF16), wo_ref[...]))
    ring_sent(0)
    ring_steps(1, 5, 5)
    h = base_ref[:, my_cols].astype(F32) + scatter_finish(0)
    gather_start(0, h)
    ring_steps(1, 6, 6)
    ring_finish(0)
    rows, gain = gather_finish(0)
    qkv = (dot_nn(rows, wbuf[0, :, :, : 3 * HD].reshape(D, 3 * HD)) * gain).astype(BF16)
    query = qkv[:, :HD]
    kvbuf[me] = qkv[:, HD:]

    def kv_copy(source, p):
        return pltpu.make_async_remote_copy(
            src_ref=kvbuf.at[source],
            dst_ref=kvbuf.at[source],
            send_sem=ks_sem.at[p],
            recv_sem=kr_sem.at[source],
            device_id={"seq": p},
            device_id_type=MESH,
        )

    def kv_send(p, carry):
        kv_copy(me, p).start()
        return carry

    def kv_recv(p, carry):
        kv_copy(p, partner).wait_recv()
        return carry

    def kv_sent(p, carry):
        kv_copy(me, p).wait_send()
        return carry

    lax.fori_loop(me + 1, NSEQ, kv_send, 0)
    ring_steps(1, 7, 8)
    ring_start(2)
    drain(crecv.at[pl.ds(0, 31)], cs_sem)
    drain(lrecv.at[pl.ds(0, 31)], ls_sem)
    ring_steps(2, 1, 4)
    lax.fori_loop(0, me, kv_recv, 0)

    kv = kvbuf[...].reshape(LATENTS, 2 * HD)
    raw = dot_nt(query, kv[:, :HD]) * SCALE
    capped = 30.0 * jnp.tanh(raw / 30.0)
    key_row = lax.broadcasted_iota(jnp.int32, (ROWS, LATENTS), 1)
    my_row = me * ROWS + lax.broadcasted_iota(jnp.int32, (ROWS, LATENTS), 0)
    expo = jnp.where(key_row <= my_row, jnp.exp(capped), 0.0)
    self_total = jnp.sum(expo, axis=1, keepdims=True)
    self_ctx = dot_nn(expo.astype(BF16), kv[:, HD:]) / self_total

    scatter_start(1, dot_nt(self_ctx.astype(BF16), wbuf[0, :, :, 3 * HD :].reshape(D, HD)))
    ring_sent(1)
    ring_steps(2, 5, 5)
    h = h + scatter_finish(1)
    gather_start(1, h)
    ring_steps(2, 6, 6)
    ring_finish(1)
    rows, gain = gather_finish(1)
    hidden = jax.nn.gelu(dot_nn(rows, weight(1)) * gain).astype(BF16)
    ring_steps(2, 7, 8)
    ring_finish(2)
    part[...] = dot_nt(hidden, weight(2))
    part[:, my_cols] += h
    for f in range(NLAT):
        fsend[f] = part[2 * f : 2 * f + 2, :]

    def last_send(i, carry):
        p = lax.rem(lme + i, NLAT)
        pltpu.make_async_remote_copy(
            src_ref=fsend.at[p],
            dst_ref=frecv.at[i],
            send_sem=fs_sem,
            recv_sem=fr_sem,
            device_id={"lat": p},
            device_id_type=MESH,
        ).start()
        return carry

    lax.fori_loop(1, NLAT, last_send, 0)
    ring_sent(2)
    for n in range(2):
        drain(rrecv.at[n, pl.ds(1, NLAT - 1)], rs_sem.at[n])
        drain(gath.at[n, pl.ds(0, NLAT - 1)], gs_sem.at[n])
    lax.fori_loop(me + 1, NSEQ, kv_sent, 0)
    drain(frecv.at[pl.ds(1, NLAT - 1)], fr_sem)
    acc = fsend[lme]
    for i in range(1, NLAT):
        acc += frecv[i]
    out_ref[...] = acc.astype(BF16)
    drain(frecv.at[pl.ds(1, NLAT - 1)], fs_sem)


def local(
    inputs,
    cross_kv,
    cross_out_w,
    latent_query,
    latent_base,
    latent_pos,
    attn_qkv,
    attn_out,
    mlp_up,
    mlp_down,
):
    dma = pltpu.SemaphoreType.DMA
    vmem = pl.BlockSpec(memory_space=pltpu.VMEM)
    hbm = pl.BlockSpec(memory_space=pl.ANY)
    w0 = jnp.concatenate([attn_qkv[0].reshape(CHUNK, 3 * HD), attn_out[0]], axis=1)
    return pl.pallas_call(
        kernel,
        out_shape=jax.ShapeDtypeStruct((ROWS // NLAT, D), BF16),
        in_specs=[hbm, hbm] + [vmem] * 7,
        out_specs=vmem,
        scratch_shapes=[
            pltpu.VMEM((TOK, D), BF16),
            pltpu.VMEM((D, 2 * HD), BF16),
            pltpu.VMEM((TOK, HD), BF16),
            pltpu.VMEM((TOK, HD), BF16),
            pltpu.VMEM((NSEQ, ROWS, HD), BF16),
            pltpu.VMEM((3, NSEQ, CHUNK, HID), BF16),
            pltpu.VMEM((NSEQ, ROWS, HD), BF16),
            pltpu.VMEM((NSEQ, ROWS, HD), BF16),
            pltpu.VMEM((8, 1, 128), F32),
            pltpu.VMEM((NSEQ, 1, 128), F32),
            pltpu.VMEM((128, 128), F32),
            pltpu.VMEM((128, 128), F32),
            pltpu.VMEM((2, NLAT, ROWS, HD), BF16),
            pltpu.VMEM((2, NLAT, ROWS, HD), BF16),
            pltpu.VMEM((2, ROWS, HD), BF16),
            pltpu.VMEM((2, NLAT, ROWS, HD), BF16),
            pltpu.VMEM((NSEQ, ROWS, 2 * HD), BF16),
            pltpu.VMEM((ROWS, D), F32),
            pltpu.VMEM((NLAT, 2, D), F32),
            pltpu.VMEM((NLAT, 2, D), F32),
            dma((2,)),
            dma,
            dma((8,)),
            dma((3,)),
            dma((3, 9)),
            dma((3, 9)),
            dma((3,)),
            dma,
            dma,
            dma,
            dma,
            dma((2,)),
            dma((2,)),
            dma((2,)),
            dma((2,)),
            dma((NSEQ,)),
            dma((NSEQ,)),
            dma,
            dma,
        ],
        compiler_params=pltpu.CompilerParams(
            collective_id=0, has_side_effects=True, vmem_limit_bytes=52 << 20
        ),
    )(
        inputs,
        cross_kv.reshape(D, 2 * HD),
        cross_out_w,
        latent_query,
        latent_base,
        latent_pos.reshape(LATENTS, 1),
        w0,
        mlp_up[0],
        mlp_down[0],
    )


def solution(mesh):
    return jax.shard_map(
        local,
        mesh=mesh,
        in_specs=(
            P("seq", None),
            P(None, None, "lat"),
            P("lat", None),
            P("seq", "lat"),
            P("seq", None),
            P(),
            P(None, "seq", None, "lat"),
            P(None, "seq", "lat"),
            P(None, "seq", "lat"),
            P(None, "seq", "lat"),
        ),
        out_specs=P(("seq", "lat"), None),
        check_vma=False,
    )
```

time: 1380 us -> 161 us (0.12)
  waiting for transfers between devices: 927 us -> 0 us
  blocking collectives: 315 us -> 0 us
  Pallas kernels: 0 us -> 150 us
  other arithmetic: 80.2 us -> 0.73 us
  local copies, waits for them, and re-layouts: 28.9 us -> 8.03 us
  matrix products: 15.9 us -> 0 us
    all_gather x4 -> x0, waiting for transfers between devices: 583 us -> none  [the longest x1 151 us: combined_all(): gathered = jax.tree.map(lambda a: lax.all_gather(a, axis), part)]
    psum x3 -> x0, waiting for transfers between devices: 342 us -> none  [add_heads(): return h + lax.psum(term, 'lat')]
    all_gather x5 -> x0, blocking collectives: 315 us -> none  [the longest x2 118 us: combined_all(): gathered = jax.tree.map(lambda a: lax.all_gather(a, axis), part)]
    pallas_call x0 -> x1, Pallas kernels: none -> 150 us  [local(): pl.pallas_call(kernel, out_shape=jax.ShapeDtypeStruct((ROWS // NLAT, D),...]
    add x64 -> x0, other arithmetic: 73.1 us -> none  [the longest x31 72.7 us: combine(): first[2] * left[:, None] + second[2] * right[:, None]]
    dynamic_slice x35 -> x0, local copies, waits for them, and re-layouts: 25.7 us -> none  [the longest x34 25.7 us: take(): lax.dynamic_index_in_dim(a, source, 0, False)]
    dot_general x8 -> x0, matrix products: 15.9 us -> none  [the longest x1 4.18 us: local(): jnp.einsum('lf,df->ld', hidden, down_w[0], preferred_element_type=jnp.flo...]
  transfers between devices with their start and end apart: 7 -> 0, of which waited for: 7 -> 0; matrix products, arithmetic and copies ran while one was open for 0% -> 0% of each run, Pallas kernels for 0% -> 0%
where the time goes in v1:
time: 161 us; the launch traced here: 159 us
  Pallas kernels  150 us (93%)
  local copies, waits for them, and re-layouts  8.03 us (5%)
    pallas_call x1, Pallas kernels, local(): pl.pallas_call(kernel, out_shape=jax.ShapeDtypeStruct((ROWS // NLAT, D),...  150 us
    unnamed x14, local copies, waits for them, and re-layouts  7.13 us

profile of v1, /device:TPU:1, one launch (start us, length us, event | category | flops | bytes accessed | tf_op | source)
XLA Modules:
  0.0 158.9 jit_solution(2038930510131205035)
XLA Ops:
  0.0 0.0 copy-start
  0.0 0.9 copy.12
  0.9 0.7 pad_maximum_fusion.w0_ref
  1.7 0.9 copy.13.pos_ref
  2.6 2.3 %copy.18 = bf16[256,8,2,128]{3,1,2,0:T(8,128)(2,1)} copy(bf16[256,8,2,128]{3,2,1,0:T(2,128)(2,1)} %bitcast.16) | data formatting | bytes 2097152
  4.9 0.0 copy-done
  4.9 0.0 copy-start.1
  4.9 0.9 copy-done.1
  5.8 0.0 copy-start.2
  5.8 0.8 copy-done.2
  6.6 0.0 copy-start.3
  6.6 0.8 copy-done.3
  7.5 0.0 copy-start.4
  7.5 0.7 copy-done.4
  8.2 150.2 %shard_map.100 = bf16[2,2048]{1,0:T(2,128)(2,1)S(1)} custom-call(bf16[768,2048]{1,0:T(8,128)(2,1)} %x_hbm.1, bf16[2048,256]{1,0:T(8,128)(2,1)} %bitcast.15, bf16[128,2048]{1,0:T(8,128)(2,1)S(1)} %copy-done, bf16[32,128]{1,0:T(8,128)(2,1)S(1)} %copy-done.4, bf16[32,2048]{1,0:T(8,128)(2,1)S(1)} %copy-done.1, s32[1024,1]{1,0:T(8,128)S(1)} %copy.13.pos_ref, ...), custom_call_target="tpu_custom_call" | custom-call | tf_op jit(solution)/shard_map/pallas_call | solution.py:455
  158.3 0.6 copy.21
  (1 shorter events, 0.0 us)
Async XLA Ops:
  0.0 4.9 %copy-start = (bf16[128,2048]{1,0:T(8,128)(2,1)S(1)}, bf16[128,2048]{1,0:T(8,128)(2,1)}, u32[]{:S(2)}) copy-start(bf16[128,2048]{1,0:T(8,128)(2,1)} %wo_ref.1) | copy-start | bytes 1572868
  4.9 0.9 copy-start.1
  5.8 0.8 copy-start.2
  6.6 0.8 copy-start.3
  7.5 0.7 copy-start.4

commit v2 on v1

v2 whole, which is shorter than its diff:
```python
import math

import jax
import jax.numpy as jnp
from jax import lax
from jax.experimental import pallas as pl
from jax.experimental.pallas import tpu as pltpu
from jax.sharding import PartitionSpec as P

HD = 128
NSEQ = 32
NZ = 16
NLAT = 16
ROWS = 32
LATENTS = 1024
TOK = 768
D = 2048
HID = 512
CHUNK = 64
MESH = pl.DeviceIdType.MESH
F32 = jnp.float32
BF16 = jnp.bfloat16
LOG2E = 1.4426950408889634
SCALE = 1.0 / math.sqrt(HD)
LOW = -1e30


def dot_nt(a, b):
    return lax.dot_general(a, b, (((1,), (1,)), ((), ())), preferred_element_type=F32)


def dot_nn(a, b):
    return jnp.dot(a, b, preferred_element_type=F32)


def kernel(
    x_hbm,
    ckv_hbm,
    wo_hbm,
    q_hbm,
    base_hbm,
    pos_hbm,
    qkv_hbm,
    ow_hbm,
    up_hbm,
    down_hbm,
    out_ref,
    xv,
    ckvv,
    wov,
    basev,
    posv,
    kvt,
    qbuf,
    wbuf0,
    wbuf1,
    part_n,
    part_m,
    part_l,
    csend,
    crecv,
    lsend,
    lrecv,
    lmat,
    ltr,
    rsend,
    rrecv,
    hsend,
    gath,
    kvbuf,
    qx,
    sx,
    rx,
    part,
    fsend,
    frecv,
    load_sem,
    qs_sem,
    qr_sem,
    xs_sem,
    xr_sem,
    ws_sem,
    wf_sem,
    wb_sem,
    wx_sem,
    cs_sem,
    cr_sem,
    ls_sem,
    lr_sem,
    rs_sem,
    rr_sem,
    gs_sem,
    gr_sem,
    ks_sem,
    kr_sem,
    ps_sem,
    pr_sem,
    fs_sem,
    fr_sem,
):
    me = lax.axis_index("seq")
    lme = lax.axis_index("lat")
    xh = me // NZ
    z = lax.rem(me, NZ)
    line = xh * NZ
    partner = lax.rem(me + NZ, NSEQ)
    my_quad = z // 4
    z_up = line + lax.rem(z + 1, NZ)
    z_down = line + lax.rem(z + NZ - 1, NZ)

    loads = [
        pltpu.make_async_copy(src, dst, load_sem.at[n])
        for n, (src, dst) in enumerate(
            (
                (q_hbm, qbuf.at[z]),
                (qkv_hbm.at[0], wbuf0.at[me, :, pl.ds(0, HD)]),
                (qkv_hbm.at[1], wbuf0.at[me, :, pl.ds(HD, HD)]),
                (qkv_hbm.at[2], wbuf0.at[me, :, pl.ds(2 * HD, HD)]),
                (ow_hbm, wbuf0.at[me, :, pl.ds(3 * HD, HD)]),
                (ckv_hbm, ckvv),
                (x_hbm, xv),
                (up_hbm, wbuf1.at[me, 0]),
                (down_hbm, wbuf1.at[me, 1]),
                (pos_hbm, posv),
                (wo_hbm, wov),
                (base_hbm, basev),
            )
        )
    ]
    for load in loads:
        load.start()

    qx[1] = jnp.zeros((ROWS, HD), BF16)
    rx[...] = jnp.zeros_like(rx)

    barrier = pltpu.get_barrier_semaphore()

    def greet(device_id):
        pl.semaphore_signal(barrier, inc=1, device_id=device_id, device_id_type=MESH)

    def in_line(i):
        return line + lax.rem(z + i, NZ)

    def in_lat(i):
        return lax.rem(lme + i, NLAT)

    def greet_all(i, carry):
        greet({"seq": in_line(i)})
        greet({"lat": in_lat(i)})
        return carry

    lax.fori_loop(1, NZ, greet_all, 0)
    greet({"seq": partner})
    for load in loads[:5]:
        load.wait()
    pl.semaphore_wait(barrier, NZ - 1 + 1 + NLAT - 1)

    def drain(ref, sem):
        pltpu.make_async_copy(ref, ref, sem).wait()

    def remote(src, dst, send_sem, recv_sem, device_id):
        return pltpu.make_async_remote_copy(
            src_ref=src,
            dst_ref=dst,
            send_sem=send_sem,
            recv_sem=recv_sem,
            device_id=device_id,
            device_id_type=MESH,
        )

    def send_query(i, carry):
        remote(qbuf.at[z], qbuf.at[z], qs_sem, qr_sem.at[my_quad], {"seq": in_line(i)}).start()
        return carry

    lax.fori_loop(1, NZ, send_query, 0)

    wbufs = (wbuf0, wbuf1)

    def move(r, src, to, recv_sem):
        chunk = wbufs[r].at[src]
        return remote(chunk, chunk, ws_sem.at[r], recv_sem, {"seq": to})

    def ring_start(r):
        move(r, me, z_up, wf_sem.at[r, 1]).start()
        move(r, me, z_down, wb_sem.at[r, 1]).start()

    def ring_step(r, k):
        low = line + lax.rem(z + NZ - k, NZ)
        high = line + lax.rem(z + k, NZ)
        move(r, low, z_up, wf_sem.at[r, k]).wait_recv()
        if k < 8:
            move(r, low, z_up, wf_sem.at[r, k + 1]).start()
            move(r, high, z_down, wb_sem.at[r, k]).wait_recv()
            if k < 7:
                move(r, high, z_down, wb_sem.at[r, k + 1]).start()
        move(r, low, partner, wx_sem.at[r]).start()
        if k < 8:
            move(r, high, partner, wx_sem.at[r]).start()

    def ring_finish(r):
        drain(wbufs[r].at[pl.ds((1 - xh) * NZ, NZ)], wx_sem.at[r])

    def ring_sent(r):
        drain(wbufs[r].at[pl.ds(0, 31)], ws_sem.at[r])

    ring_start(0)

    loads[5].wait()
    loads[6].wait()
    half_rows = TOK // 2
    for half in range(2):
        rows = pl.ds(half * half_rows, half_rows)
        kvt[0, rows, :] = dot_nn(xv[rows, :], ckvv[...]).astype(BF16)
        remote(kvt.at[0, rows], kvt.at[1, rows], xs_sem, xr_sem, {"seq": partner}).start()
    move(0, me, partner, wx_sem.at[0]).start()
    for load in loads[7:]:
        load.wait()
    ring_step(0, 1)

    def attend(quad, slot, owner):
        q = qbuf[pl.ds(quad * 4, 4)].reshape(4 * ROWS, HD)
        scores = dot_nt(q, kvt[slot, :, :HD])
        row = posv[pl.ds(xh * 4 + quad, 1), :].astype(F32)
        pos = jnp.broadcast_to(row, (128, 128)).T[:, 0:1]
        key = lax.broadcasted_iota(jnp.int32, (1, TOK), 1) + owner * TOK
        allowed = key.astype(F32) <= pos
        top = jnp.max(jnp.where(allowed, scores, LOW), axis=1, keepdims=True)
        weights = jnp.where(allowed, jnp.exp2((scores - top) * (SCALE * LOG2E)), 0.0)
        total = jnp.sum(weights, axis=1, keepdims=True)
        numer = dot_nn(weights.astype(BF16), kvt[slot, :, HD:])
        return top, total, numer

    def first_pass(j, carry):
        quad = lax.rem(my_quad + j, 4)

        @pl.when(j == 0)
        def _():
            drain(qbuf.at[pl.ds(0, 3)], qr_sem.at[quad])

        @pl.when(j > 0)
        def _():
            drain(qbuf.at[pl.ds(0, 4)], qr_sem.at[quad])

        top, total, numer = attend(quad, 0, me)
        part_n[quad] = numer
        part_m[quad] = jnp.broadcast_to(top, (128, 128))
        part_l[quad] = jnp.broadcast_to(total, (128, 128))
        return carry

    def second_pass(j, carry):
        quad = lax.rem(my_quad + j, 4)
        top, total, numer = attend(quad, 1, partner)
        top_1 = part_m[quad]
        best = jnp.maximum(top_1, top)
        left = jnp.exp2((top_1 - best) * (SCALE * LOG2E))
        right = jnp.exp2((top - best) * (SCALE * LOG2E))
        total = part_l[quad] * left + total * right
        some = total > 0.0
        safe = jnp.where(some, total, 1.0)
        ctx = (part_n[quad] * left + numer * right) / safe
        lse = jnp.where(some, best * (SCALE * LOG2E) + jnp.log2(safe), LOW)
        csend[pl.ds(quad * 4, 4)] = ctx.astype(BF16).reshape(4, ROWS, HD)
        lsend[quad] = lse.T[0:1, :]

        def send_part(t, carry):
            p = quad * 4 + t

            @pl.when(p != z)
            def _():
                to = {"seq": line + p}
                remote(csend.at[p], crecv.at[z], cs_sem, cr_sem, to).start()
                remote(lsend.at[quad], lrecv.at[z], ls_sem, lr_sem, to).start()

            return carry

        lax.fori_loop(0, 4, send_part, 0)
        return carry

    lax.fori_loop(0, 2, first_pass, 0)
    ring_step(0, 2)
    lax.fori_loop(2, 4, first_pass, 0)
    ring_step(0, 3)
    drain(kvt.at[1], xr_sem)
    lax.fori_loop(0, 2, second_pass, 0)
    ring_step(0, 4)
    lax.fori_loop(2, 4, second_pass, 0)
    ring_step(0, 5)
    ring_start(1)
    crecv[z] = csend[z]
    lrecv[z] = lsend[my_quad]
    drain(qbuf.at[pl.ds(0, 15)], qs_sem)
    drain(kvt.at[0], xs_sem)
    ring_step(0, 6)
    ring_step(0, 7)
    drain(crecv.at[pl.ds(0, 15)], cr_sem)
    drain(lrecv.at[pl.ds(0, 15)], lr_sem)

    lmat[...] = jnp.zeros((128, 128), F32)
    for s in range(NZ):
        lmat[s : s + 1, :] = lrecv[s]
    logs = lmat[0:NZ, :]
    share = jnp.exp2(logs - jnp.max(logs, axis=0, keepdims=True))
    lmat[0:NZ, :] = share / jnp.sum(share, axis=0, keepdims=True)
    ltr[...] = lmat[...].T
    mine = ltr[pl.ds(pl.multiple_of(lax.rem(z, 4) * ROWS, ROWS), ROWS), :]
    context = jnp.zeros((ROWS, HD), F32)
    for s in range(NZ):
        context += mine[:, s : s + 1] * crecv[s].astype(F32)

    def scatter_start(n, term):
        for f in range(NLAT):
            rsend[n, f] = term[:, f * HD : (f + 1) * HD].astype(BF16)

        def send(i, carry):
            p = in_lat(i)
            remote(rsend.at[n, p], rrecv.at[n, i], rs_sem.at[n], rr_sem.at[n], {"lat": p}).start()
            return carry

        lax.fori_loop(1, NLAT, send, 0)

    def scatter_finish(n):
        drain(rrecv.at[n, pl.ds(1, NLAT - 1)], rr_sem.at[n])
        acc = rsend[n, lme].astype(F32)
        for i in range(1, NLAT):
            acc += rrecv[n, i].astype(F32)
        return acc

    def gather_start(n, h):
        hsend[n] = h.astype(BF16)
        gath[n, lme] = h.astype(BF16)

        def send(i, carry):
            to = {"lat": in_lat(i)}
            remote(hsend.at[n], gath.at[n, lme], gs_sem.at[n], gr_sem.at[n], to).start()
            return carry

        lax.fori_loop(1, NLAT, send, 0)

    def gather_finish(n):
        drain(gath.at[n, pl.ds(0, NLAT - 1)], gr_sem.at[n])
        rows = jnp.concatenate([gath[n, f] for f in range(NLAT)], axis=1)
        wide = rows.astype(F32)
        gain = lax.rsqrt(jnp.mean(wide * wide, axis=-1, keepdims=True) + 1e-06)
        return rows, gain

    my_cols = pl.ds(pl.multiple_of(lme * HD, HD), HD)
    scatter_start(0, dot_nn(context.astype(BF16), wov[...]))
    ring_step(0, 8)
    move(1, me, partner, wx_sem.at[1]).start()
    h = basev[:, my_cols].astype(F32) + scatter_finish(0)
    gather_start(0, h)
    ring_step(1, 1)
    ring_sent(0)
    ring_finish(0)
    rows, gain = gather_finish(0)
    qkv = (dot_nn(rows, wbuf0[:, :, : 3 * HD].reshape(D, 3 * HD)) * gain).astype(BF16)
    qx[0] = qkv[:, :HD]
    kvbuf[z] = qkv[:, HD:]

    query_out = remote(qx.at[0], qx.at[1], ps_sem.at[0], pr_sem.at[0], {"seq": partner})
    result_out = remote(sx, rx, ps_sem.at[1], pr_sem.at[1], {"seq": partner})

    def kv_send(i, carry):
        remote(kvbuf.at[z], kvbuf.at[z], ks_sem, kr_sem, {"seq": in_line(i)}).start()
        return carry

    lax.fori_loop(1, NZ, kv_send, 0)

    @pl.when(xh == 1)
    def _():
        query_out.start()

    drain(crecv.at[pl.ds(0, 15)], cs_sem)
    drain(lrecv.at[pl.ds(0, 15)], ls_sem)
    ring_step(1, 2)
    ring_step(1, 3)

    @pl.when(xh == 0)
    def _():
        query_out.wait_recv()

    drain(kvbuf.at[pl.ds(0, 15)], kr_sem)
    line_rows = NZ * ROWS
    raw = dot_nt(qx[...].reshape(2 * ROWS, HD), kvbuf[:, :, :HD].reshape(line_rows, HD)) * SCALE
    capped = 30.0 * jnp.tanh(raw / 30.0)
    key_row = lax.broadcasted_iota(jnp.int32, (2 * ROWS, line_rows), 1)
    row = lax.broadcasted_iota(jnp.int32, (2 * ROWS, line_rows), 0)
    seen = (key_row <= z * ROWS + row) | (row >= ROWS)
    expo = jnp.where(seen, jnp.exp(capped), 0.0)
    self_total = jnp.sum(expo, axis=1, keepdims=True)
    self_numer = dot_nn(expo.astype(BF16), kvbuf[:, :, HD:].reshape(line_rows, HD))

    @pl.when(xh == 0)
    def _():
        sx[0:ROWS, :] = self_numer[ROWS:, :]
        sx[ROWS:, :] = jnp.broadcast_to(self_total[ROWS:, :], (ROWS, HD))
        result_out.start()

    ring_step(1, 4)

    @pl.when(xh == 1)
    def _():
        result_out.wait_recv()

    self_ctx = (self_numer[0:ROWS, :] + rx[0:ROWS, :]) / (self_total[0:ROWS, :] + rx[ROWS:, :])

    scatter_start(1, dot_nt(self_ctx.astype(BF16), wbuf0[:, :, 3 * HD :].reshape(D, HD)))
    ring_step(1, 5)
    h = h + scatter_finish(1)
    gather_start(1, h)
    ring_step(1, 6)
    ring_step(1, 7)
    ring_step(1, 8)
    ring_finish(1)
    rows, gain = gather_finish(1)
    hidden = jax.nn.gelu(dot_nn(rows, wbuf1[:, 0].reshape(D, HID)) * gain).astype(BF16)
    part[...] = dot_nt(hidden, wbuf1[:, 1].reshape(D, HID))
    part[:, my_cols] += h
    for f in range(NLAT):
        fsend[f] = part[2 * f : 2 * f + 2, :]

    def last_send(i, carry):
        p = in_lat(i)
        remote(fsend.at[p], frecv.at[i], fs_sem, fr_sem, {"lat": p}).start()
        return carry

    lax.fori_loop(1, NLAT, last_send, 0)
    ring_sent(1)
    for n in range(2):
        drain(rrecv.at[n, pl.ds(1, NLAT - 1)], rs_sem.at[n])
        drain(gath.at[n, pl.ds(0, NLAT - 1)], gs_sem.at[n])
    drain(kvbuf.at[pl.ds(0, 15)], ks_sem)

    @pl.when(xh == 1)
    def _():
        query_out.wait_send()

    @pl.when(xh == 0)
    def _():
        result_out.wait_send()

    drain(frecv.at[pl.ds(1, NLAT - 1)], fr_sem)
    acc = fsend[lme]
    for i in range(1, NLAT):
        acc += frecv[i]
    out_ref[...] = acc.astype(BF16)
    drain(frecv.at[pl.ds(1, NLAT - 1)], fs_sem)


def local(
    inputs,
    cross_kv,
    cross_out_w,
    latent_query,
    latent_base,
    latent_pos,
    attn_qkv,
    attn_out,
    mlp_up,
    mlp_down,
):
    dma = pltpu.SemaphoreType.DMA
    vmem = pl.BlockSpec(memory_space=pltpu.VMEM)
    hbm = pl.BlockSpec(memory_space=pltpu.HBM)
    return pl.pallas_call(
        kernel,
        out_shape=jax.ShapeDtypeStruct((ROWS // NLAT, D), BF16),
        in_specs=[hbm] * 10,
        out_specs=vmem,
        scratch_shapes=[
            pltpu.VMEM((TOK, D), BF16),
            pltpu.VMEM((D, 2 * HD), BF16),
            pltpu.VMEM((HD, D), BF16),
            pltpu.VMEM((ROWS, D), BF16),
            pltpu.VMEM((8, 128), jnp.int32),
            pltpu.VMEM((2, TOK, 2 * HD), BF16),
            pltpu.VMEM((NZ, ROWS, HD), BF16),
            pltpu.VMEM((NSEQ, CHUNK, HID), BF16),
            pltpu.VMEM((NSEQ, 2, CHUNK, HID), BF16),
            pltpu.VMEM((4, 128, 128), F32),
            pltpu.VMEM((4, 128, 128), F32),
            pltpu.VMEM((4, 128, 128), F32),
            pltpu.VMEM((NZ, ROWS, HD), BF16),
            pltpu.VMEM((NZ, ROWS, HD), BF16),
            pltpu.VMEM((4, 1, 128), F32),
            pltpu.VMEM((NZ, 1, 128), F32),
            pltpu.VMEM((128, 128), F32),
            pltpu.VMEM((128, 128), F32),
            pltpu.VMEM((2, NLAT, ROWS, HD), BF16),
            pltpu.VMEM((2, NLAT, ROWS, HD), BF16),
            pltpu.VMEM((2, ROWS, HD), BF16),
            pltpu.VMEM((2, NLAT, ROWS, HD), BF16),
            pltpu.VMEM((NZ, ROWS, 2 * HD), BF16),
            pltpu.VMEM((2, ROWS, HD), BF16),
            pltpu.VMEM((2 * ROWS, HD), F32),
            pltpu.VMEM((2 * ROWS, HD), F32),
            pltpu.VMEM((ROWS, D), F32),
            pltpu.VMEM((NLAT, 2, D), F32),
            pltpu.VMEM((NLAT, 2, D), F32),
            dma((12,)),
            dma,
            dma((4,)),
            dma,
            dma,
            dma((2,)),
            dma((2, 9)),
            dma((2, 9)),
            dma((2,)),
            dma,
            dma,
            dma,
            dma,
            dma((2,)),
            dma((2,)),
            dma((2,)),
            dma((2,)),
            dma,
            dma,
            dma((2,)),
            dma((2,)),
            dma,
            dma,
        ],
        compiler_params=pltpu.CompilerParams(
            collective_id=0, has_side_effects=True, vmem_limit_bytes=63 << 20
        ),
    )(
        inputs,
        cross_kv.reshape(D, 2 * HD),
        cross_out_w,
        latent_query,
        latent_base,
        latent_pos.reshape(8, 128),
        jnp.swapaxes(attn_qkv[0], 0, 1),
        attn_out[0],
        mlp_up[0],
        mlp_down[0],
    )


def solution(mesh):
    return jax.shard_map(
        local,
        mesh=mesh,
        in_specs=(
            P("seq", None),
            P(None, None, "lat"),
            P("lat", None),
            P("seq", "lat"),
            P("seq", None),
            P(),
            P(None, "seq", None, "lat"),
            P(None, "seq", "lat"),
            P(None, "seq", "lat"),
            P(None, "seq", "lat"),
        ),
        out_specs=P(("seq", "lat"), None),
        check_vma=False,
    )
```

time: 161 us -> 128 us (0.80)
  Pallas kernels: 150 us -> 124 us
  local copies, waits for them, and re-layouts: 8.03 us -> 3.65 us
    pallas_call x1, Pallas kernels: 150 us -> 124 us  [local(): pl.pallas_call(kernel, out_shape=jax.ShapeDtypeStruct((ROWS // NLAT, D),...]
    unnamed x14 -> x2, local copies, waits for them, and re-layouts: 7.13 us -> 3.65 us
where the time goes in v2:
time: 128 us; the launch traced here: 127 us
  Pallas kernels  124 us (97%)
  local copies, waits for them, and re-layouts  3.65 us (3%)
    pallas_call x1, Pallas kernels, local(): pl.pallas_call(kernel, out_shape=jax.ShapeDtypeStruct((ROWS // NLAT, D),...  124 us
    unnamed x2, local copies, waits for them, and re-layouts  3.65 us

profile of v2, /device:TPU:1, one launch (start us, length us, event | category | flops | bytes accessed | tf_op | source)
XLA Modules:
  0.0 127.4 jit_solution(8618916396975346022)
XLA Ops:
  0.0 2.4 %copy.13 = bf16[256,8,2,128]{3,1,2,0:T(8,128)(2,1)} copy(bf16[256,8,2,128]{3,2,1,0:T(2,128)(2,1)} %bitcast.12) | data formatting | bytes 2097152
  2.4 123.8 %shard_map.100 = bf16[2,2048]{1,0:T(2,128)(2,1)} custom-call(bf16[768,2048]{1,0:T(8,128)(2,1)} %x_hbm.1, bf16[2048,256]{1,0:T(8,128)(2,1)} %bitcast.11, bf16[128,2048]{1,0:T(8,128)(2,1)} %wo_hbm.1, bf16[32,128]{1,0:T(8,128)(2,1)} %q_hbm.1, bf16[32,2048]{1,0:T(8,128)(2,1)} %base_hbm.1, s32[8,128]{1,0:T(8,128)} %bitcast.17, bf16[3,64,128]{2,1,0:T(8,128)(2,1)} %bitcast.15, ...), custom_call_target="tpu_custom_call" | custom-call | tf_op jit(solution)/shard_map/pallas_call | solution.py:465
  126.1 1.3 %copy.15 = bf16[2,2048]{1,0:T(2,128)(2,1)} copy(bf16[2,2048]{1,0:T(2,128)(2,1)} %shard_map.100) | data formatting | bytes 16384

commit v3 on v2

--- a/solution.py
+++ b/solution.py
@@ -71,6 +71,9 @@
     qx,
     sx,
     rx,
+    wide_in,
+    up_out,
+    up_in,
     part,
     fsend,
     frecv,
@@ -119,8 +122,8 @@
                 (ow_hbm, wbuf0.at[me, :, pl.ds(3 * HD, HD)]),
                 (ckv_hbm, ckvv),
                 (x_hbm, xv),
-                (up_hbm, wbuf1.at[me, 0]),
-                (down_hbm, wbuf1.at[me, 1]),
+                (up_hbm, wbuf1.at[z, 0]),
+                (down_hbm, wbuf1.at[z, 1]),
                 (pos_hbm, posv),
                 (wo_hbm, wov),
                 (base_hbm, basev),
@@ -130,9 +133,6 @@
     for load in loads:
         load.start()
 
-    qx[1] = jnp.zeros((ROWS, HD), BF16)
-    rx[...] = jnp.zeros_like(rx)
-
     barrier = pltpu.get_barrier_semaphore()
 
     def greet(device_id):
@@ -147,13 +147,16 @@
     def greet_all(i, carry):
         greet({"seq": in_line(i)})
         greet({"lat": in_lat(i)})
+        greet({"seq": partner, "lat": in_lat(i)})
         return carry
 
     lax.fori_loop(1, NZ, greet_all, 0)
+    qx[1] = jnp.zeros((ROWS, HD), BF16)
+    rx[...] = jnp.zeros_like(rx)
     greet({"seq": partner})
     for load in loads[:5]:
         load.wait()
-    pl.semaphore_wait(barrier, NZ - 1 + 1 + NLAT - 1)
+    pl.semaphore_wait(barrier, NZ - 1 + 1 + 2 * (NLAT - 1))
 
     def drain(ref, sem):
         pltpu.make_async_copy(ref, ref, sem).wait()
@@ -174,34 +177,31 @@
 
     lax.fori_loop(1, NZ, send_query, 0)
 
-    wbufs = (wbuf0, wbuf1)
-
-    def move(r, src, to, recv_sem):
-        chunk = wbufs[r].at[src]
-        return remote(chunk, chunk, ws_sem.at[r], recv_sem, {"seq": to})
+    def chunk(r, place):
+        return wbuf0.at[line + place] if r == 0 else wbuf1.at[place]
+
+    def move(r, place, to, recv_sem):
+        ref = chunk(r, place)
+        return remote(ref, ref, ws_sem.at[r], recv_sem, {"seq": to})
 
     def ring_start(r):
-        move(r, me, z_up, wf_sem.at[r, 1]).start()
-        move(r, me, z_down, wb_sem.at[r, 1]).start()
+        move(r, z, z_up, wf_sem.at[r, 1]).start()
+        move(r, z, z_down, wb_sem.at[r, 1]).start()
 
     def ring_step(r, k):
-        low = line + lax.rem(z + NZ - k, NZ)
-        high = line + lax.rem(z + k, NZ)
+        low = lax.rem(z + NZ - k, NZ)
+        high = lax.rem(z + k, NZ)
         move(r, low, z_up, wf_sem.at[r, k]).wait_recv()
         if k < 8:
             move(r, low, z_up, wf_sem.at[r, k + 1]).start()
             move(r, high, z_down, wb_sem.at[r, k]).wait_recv()
             if k < 7:
                 move(r, high, z_down, wb_sem.at[r, k + 1]).start()
-        move(r, low, partner, wx_sem.at[r]).start()
-        if k < 8:
-            move(r, high, partner, wx_sem.at[r]).start()
-
-    def ring_finish(r):
-        drain(wbufs[r].at[pl.ds((1 - xh) * NZ, NZ)], wx_sem.at[r])
-
-    def ring_sent(r):
-        drain(wbufs[r].at[pl.ds(0, 31)], ws_sem.at[r])
+
+    def cross(k):
+        move(0, lax.rem(z + NZ - k, NZ), partner, wx_sem).start()
+        if 0 < k < 8:
+            move(0, lax.rem(z + k, NZ), partner, wx_sem).start()
 
     ring_start(0)
 
@@ -212,7 +212,6 @@
         rows = pl.ds(half * half_rows, half_rows)
         kvt[0, rows, :] = dot_nn(xv[rows, :], ckvv[...]).astype(BF16)
         remote(kvt.at[0, rows], kvt.at[1, rows], xs_sem, xr_sem, {"seq": partner}).start()
-    move(0, me, partner, wx_sem.at[0]).start()
     for load in loads[7:]:
         load.wait()
     ring_step(0, 1)
@@ -281,17 +280,27 @@
     lax.fori_loop(2, 4, first_pass, 0)
     ring_step(0, 3)
     drain(kvt.at[1], xr_sem)
+    for k in range(3):
+        cross(k)
     lax.fori_loop(0, 2, second_pass, 0)
     ring_step(0, 4)
+    cross(3)
     lax.fori_loop(2, 4, second_pass, 0)
     ring_step(0, 5)
+    cross(4)
     ring_start(1)
     crecv[z] = csend[z]
     lrecv[z] = lsend[my_quad]
     drain(qbuf.at[pl.ds(0, 15)], qs_sem)
     drain(kvt.at[0], xs_sem)
     ring_step(0, 6)
+    cross(5)
     ring_step(0, 7)
+    cross(6)
+    ring_step(0, 8)
+    cross(7)
+    cross(8)
+    ring_step(1, 1)
     drain(crecv.at[pl.ds(0, 15)], cr_sem)
     drain(lrecv.at[pl.ds(0, 15)], lr_sem)
 
@@ -325,34 +334,32 @@
             acc += rrecv[n, i].astype(F32)
         return acc
 
-    def gather_start(n, h):
-        hsend[n] = h.astype(BF16)
-        gath[n, lme] = h.astype(BF16)
+    def gather_start(h):
+        hsend[0] = h.astype(BF16)
+        gath[lme] = h.astype(BF16)
 
         def send(i, carry):
             to = {"lat": in_lat(i)}
-            remote(hsend.at[n], gath.at[n, lme], gs_sem.at[n], gr_sem.at[n], to).start()
+            remote(hsend.at[0], gath.at[lme], gs_sem.at[0], gr_sem.at[0], to).start()
             return carry
 
         lax.fori_loop(1, NLAT, send, 0)
 
-    def gather_finish(n):
-        drain(gath.at[n, pl.ds(0, NLAT - 1)], gr_sem.at[n])
-        rows = jnp.concatenate([gath[n, f] for f in range(NLAT)], axis=1)
-        wide = rows.astype(F32)
-        gain = lax.rsqrt(jnp.mean(wide * wide, axis=-1, keepdims=True) + 1e-06)
-        return rows, gain
+    def gather_finish():
+        drain(gath.at[pl.ds(0, NLAT - 1)], gr_sem.at[0])
+        return jnp.concatenate([gath[f] for f in range(NLAT)], axis=1)
 
     my_cols = pl.ds(pl.multiple_of(lme * HD, HD), HD)
     scatter_start(0, dot_nn(context.astype(BF16), wov[...]))
-    ring_step(0, 8)
-    move(1, me, partner, wx_sem.at[1]).start()
+    ring_step(1, 2)
     h = basev[:, my_cols].astype(F32) + scatter_finish(0)
-    gather_start(0, h)
-    ring_step(1, 1)
-    ring_sent(0)
-    ring_finish(0)
-    rows, gain = gather_finish(0)
+    gather_start(h)
+    ring_step(1, 3)
+    drain(wbuf0.at[pl.ds(0, 31)], ws_sem.at[0])
+    drain(wbuf0.at[pl.ds((1 - xh) * NZ, NZ)], wx_sem)
+    rows = gather_finish()
+    wide = rows.astype(F32)
+    gain = lax.rsqrt(jnp.mean(wide * wide, axis=-1, keepdims=True) + 1e-06)
     qkv = (dot_nn(rows, wbuf0[:, :, : 3 * HD].reshape(D, 3 * HD)) * gain).astype(BF16)
     qx[0] = qkv[:, :HD]
     kvbuf[z] = qkv[:, HD:]
@@ -360,11 +367,12 @@
     query_out = remote(qx.at[0], qx.at[1], ps_sem.at[0], pr_sem.at[0], {"seq": partner})
     result_out = remote(sx, rx, ps_sem.at[1], pr_sem.at[1], {"seq": partner})
 
-    def kv_send(i, carry):
-        remote(kvbuf.at[z], kvbuf.at[z], ks_sem, kr_sem, {"seq": in_line(i)}).start()
-        return carry
-
-    lax.fori_loop(1, NZ, kv_send, 0)
+    def kv_move(place, i, n):
+        ref = kvbuf.at[lax.rem(place, NZ)]
+        return remote(ref, ref, ks_sem, kr_sem.at[n], {"seq": in_line(i)})
+
+    for i in (4, 12, 1, 15, 2, 14, 3, 13):
+        kv_move(z, i, {4: 1, 12: 2}.get(i, 0)).start()
 
     @pl.when(xh == 1)
     def _():
@@ -372,14 +380,20 @@
 
     drain(crecv.at[pl.ds(0, 15)], cs_sem)
     drain(lrecv.at[pl.ds(0, 15)], ls_sem)
-    ring_step(1, 2)
-    ring_step(1, 3)
+    kv_move(z + 12, 4, 1).wait_recv()
+    for i in range(1, 5):
+        kv_move(z + 12, i, 0).start()
+    kv_move(z + 4, 12, 2).wait_recv()
+    for i in range(13, 16):
+        kv_move(z + 4, i, 0).start()
+    ring_step(1, 4)
+    ring_step(1, 5)
 
     @pl.when(xh == 0)
     def _():
         query_out.wait_recv()
 
-    drain(kvbuf.at[pl.ds(0, 15)], kr_sem)
+    drain(kvbuf.at[pl.ds(0, 13)], kr_sem.at[0])
     line_rows = NZ * ROWS
     raw = dot_nt(qx[...].reshape(2 * ROWS, HD), kvbuf[:, :, :HD].reshape(line_rows, HD)) * SCALE
     capped = 30.0 * jnp.tanh(raw / 30.0)
@@ -396,7 +410,7 @@
         sx[ROWS:, :] = jnp.broadcast_to(self_total[ROWS:, :], (ROWS, HD))
         result_out.start()
 
-    ring_step(1, 4)
+    ring_step(1, 6)
 
     @pl.when(xh == 1)
     def _():
@@ -405,31 +419,80 @@
     self_ctx = (self_numer[0:ROWS, :] + rx[0:ROWS, :]) / (self_total[0:ROWS, :] + rx[ROWS:, :])
 
     scatter_start(1, dot_nt(self_ctx.astype(BF16), wbuf0[:, :, 3 * HD :].reshape(D, HD)))
-    ring_step(1, 5)
+    ring_step(1, 7)
     h = h + scatter_finish(1)
-    gather_start(1, h)
-    ring_step(1, 6)
-    ring_step(1, 7)
+
+    home = lme // 8
+    col = lax.rem(lme, 8)
+    at_home = xh == home
+    hsend[1] = h.astype(BF16)
+
+    def wide_send(i, carry):
+        @pl.when(jnp.logical_or(i != lme, xh != home))
+        def _():
+            to = {"seq": home * NZ + z, "lat": i}
+            remote(hsend.at[1], wide_in.at[xh, col], gs_sem.at[1], gr_sem.at[1], to).start()
+
+        return carry
+
+    def wide_wait(sem):
+        @pl.when(at_home)
+        def _():
+            drain(gath.at[pl.ds(0, 15)], sem)
+
+        @pl.when(jnp.logical_not(at_home))
+        def _():
+            drain(gath.at[pl.ds(0, 16)], sem)
+
+    lax.fori_loop(0, NLAT, wide_send, 0)
+
+    @pl.when(at_home)
+    def _():
+        wide_in[xh, col] = hsend[1]
+
     ring_step(1, 8)
-    ring_finish(1)
-    rows, gain = gather_finish(1)
-    hidden = jax.nn.gelu(dot_nn(rows, wbuf1[:, 0].reshape(D, HID)) * gain).astype(BF16)
-    part[...] = dot_nt(hidden, wbuf1[:, 1].reshape(D, HID))
-    part[:, my_cols] += h
-    for f in range(NLAT):
-        fsend[f] = part[2 * f : 2 * f + 2, :]
-
-    def last_send(i, carry):
-        p = in_lat(i)
-        remote(fsend.at[p], frecv.at[i], fs_sem, fr_sem, {"lat": p}).start()
-        return carry
-
-    lax.fori_loop(1, NLAT, last_send, 0)
-    ring_sent(1)
+    wide_wait(gr_sem.at[1])
+    rows = jnp.concatenate([wide_in[:, f].reshape(2 * ROWS, HD) for f in range(8)], axis=1)
+    wide = rows.astype(F32)
+    square = jnp.sum(wide * wide, axis=-1, keepdims=True)
+    up = dot_nn(rows, wbuf1[:, 0].reshape(D // 2, HID))
+    up_out[:, 0:HID] = up.astype(BF16)
+    high = jnp.broadcast_to(square, (2 * ROWS, HD)).astype(BF16).astype(F32)
+    lane = lax.broadcasted_iota(jnp.int32, (2 * ROWS, HD), 1)
+    up_out[:, HID:] = jnp.where(lane < HD // 2, high, square - high).astype(BF16)
+    half_out = remote(up_out, up_in, ps_sem.at[2], pr_sem.at[2], {"seq": partner})
+    half_out.start()
+    drain(wbuf1.at[pl.ds(0, 15)], ws_sem.at[1])
     for n in range(2):
         drain(rrecv.at[n, pl.ds(1, NLAT - 1)], rs_sem.at[n])
-        drain(gath.at[n, pl.ds(0, NLAT - 1)], gs_sem.at[n])
+    drain(gath.at[pl.ds(0, NLAT - 1)], gs_sem.at[0])
+    wide_wait(gs_sem.at[1])
     drain(kvbuf.at[pl.ds(0, 15)], ks_sem)
+    half_out.wait_recv()
+    other = up_in[:, HID:].astype(F32)
+    square = square + other[:, 0:1] + other[:, HD // 2 : HD // 2 + 1]
+    gain = lax.rsqrt(square * (1.0 / D) + 1e-06)
+    hidden = jax.nn.gelu((up + up_in[:, 0:HID].astype(F32)) * gain).astype(BF16)
+    part[...] = dot_nt(hidden, wbuf1[:, 1].reshape(D // 2, HID))
+
+    @pl.when(at_home)
+    def _():
+        cols = pl.ds(pl.multiple_of(col * HD, HD), HD)
+        part[:, cols] += wide_in[:, col].reshape(2 * ROWS, HD).astype(F32)
+
+    for f in range(2 * NLAT):
+        fsend[f] = part[2 * f : 2 * f + 2, :]
+    mine = xh * NLAT + lme
+
+    def last_send(i, carry):
+        p = lax.rem(mine + i, 2 * NLAT)
+        to = {"seq": (p // NLAT) * NZ + z, "lat": lax.rem(p, NLAT)}
+        remote(fsend.at[p], frecv.at[mine], fs_sem, fr_sem, to).start()
+        return carry
+
+    lax.fori_loop(1, 2 * NLAT, last_send, 0)
+    frecv[mine] = fsend[mine]
+    half_out.wait_send()
 
     @pl.when(xh == 1)
     def _():
@@ -439,12 +502,13 @@
     def _():
         result_out.wait_send()
 
-    drain(frecv.at[pl.ds(1, NLAT - 1)], fr_sem)
-    acc = fsend[lme]
-    for i in range(1, NLAT):
-        acc += frecv[i]
-    out_ref[...] = acc.astype(BF16)
-    drain(frecv.at[pl.ds(1, NLAT - 1)], fs_sem)
+    drain(frecv.at[pl.ds(0, 31)], fr_sem)
+    for half in range(2):
+        acc = frecv[half * NLAT]
+        for i in range(1, NLAT):
+            acc += frecv[half * NLAT + i]
+        out_ref[:, half * (D // 2) : (half + 1) * (D // 2)] = acc.astype(BF16)
+    drain(frecv.at[pl.ds(0, 31)], fs_sem)
 
 
 def local(
@@ -476,7 +540,7 @@
             pltpu.VMEM((2, TOK, 2 * HD), BF16),
             pltpu.VMEM((NZ, ROWS, HD), BF16),
             pltpu.VMEM((NSEQ, CHUNK, HID), BF16),
-            pltpu.VMEM((NSEQ, 2, CHUNK, HID), BF16),
+            pltpu.VMEM((NZ, 2, CHUNK, HID), BF16),
             pltpu.VMEM((4, 128, 128), F32),
             pltpu.VMEM((4, 128, 128), F32),
             pltpu.VMEM((4, 128, 128), F32),
@@ -489,14 +553,17 @@
             pltpu.VMEM((2, NLAT, ROWS, HD), BF16),
             pltpu.VMEM((2, NLAT, ROWS, HD), BF16),
             pltpu.VMEM((2, ROWS, HD), BF16),
-            pltpu.VMEM((2, NLAT, ROWS, HD), BF16),
+            pltpu.VMEM((NLAT, ROWS, HD), BF16),
             pltpu.VMEM((NZ, ROWS, 2 * HD), BF16),
             pltpu.VMEM((2, ROWS, HD), BF16),
             pltpu.VMEM((2 * ROWS, HD), F32),
             pltpu.VMEM((2 * ROWS, HD), F32),
-            pltpu.VMEM((ROWS, D), F32),
-            pltpu.VMEM((NLAT, 2, D), F32),
-            pltpu.VMEM((NLAT, 2, D), F32),
+            pltpu.VMEM((2, 8, ROWS, HD), BF16),
+            pltpu.VMEM((2 * ROWS, HID + HD), BF16),
+            pltpu.VMEM((2 * ROWS, HID + HD), BF16),
+            pltpu.VMEM((2 * ROWS, D // 2), F32),
+            pltpu.VMEM((2 * NLAT, 2, D // 2), F32),
+            pltpu.VMEM((2 * NLAT, 2, D // 2), F32),
             dma((12,)),
             dma,
             dma((4,)),
@@ -505,7 +572,7 @@
             dma((2,)),
             dma((2, 9)),
             dma((2, 9)),
-            dma((2,)),
+            dma,
             dma,
             dma,
             dma,
@@ -515,9 +582,9 @@
             dma((2,)),
             dma((2,)),
             dma,
-            dma,
-            dma((2,)),
-            dma((2,)),
+            dma((3,)),
+            dma((3,)),
+            dma((3,)),
             dma,
             dma,
         ],

time: 128 us -> 111 us (0.87)
  Pallas kernels: 124 us -> 107 us
    pallas_call x1, Pallas kernels: 124 us -> 107 us  [local(): pl.pallas_call(kernel, out_shape=jax.ShapeDtypeStruct((ROWS // NLAT, D),...]
where the time goes in v3:
time: 111 us; the launch traced here: 110 us
  Pallas kernels  107 us (96%)
  local copies, waits for them, and re-layouts  3.65 us (3%)
    pallas_call x1, Pallas kernels, local(): pl.pallas_call(kernel, out_shape=jax.ShapeDtypeStruct((ROWS // NLAT, D),...  107 us
    unnamed x2, local copies, waits for them, and re-layouts  3.65 us

profile of v3, /device:TPU:1, one launch (start us, length us, event | category | flops | bytes accessed | tf_op | source)
XLA Modules:
  0.0 110.4 jit_solution(12960977678016709849)
XLA Ops:
  0.0 2.4 %copy.13 = bf16[256,8,2,128]{3,1,2,0:T(8,128)(2,1)} copy(bf16[256,8,2,128]{3,2,1,0:T(2,128)(2,1)} %bitcast.12) | data formatting | bytes 2097152
  2.4 106.7 %shard_map.100 = bf16[2,2048]{1,0:T(2,128)(2,1)} custom-call(bf16[768,2048]{1,0:T(8,128)(2,1)} %x_hbm.1, bf16[2048,256]{1,0:T(8,128)(2,1)} %bitcast.11, bf16[128,2048]{1,0:T(8,128)(2,1)} %wo_hbm.1, bf16[32,128]{1,0:T(8,128)(2,1)} %q_hbm.1, bf16[32,2048]{1,0:T(8,128)(2,1)} %base_hbm.1, s32[8,128]{1,0:T(8,128)} %bitcast.17, bf16[3,64,128]{2,1,0:T(8,128)(2,1)} %bitcast.15, ...), custom_call_target="tpu_custom_call" | custom-call | tf_op jit(solution)/shard_map/pallas_call | solution.py:529
  109.1 1.3 %copy.15 = bf16[2,2048]{1,0:T(2,128)(2,1)} copy(bf16[2,2048]{1,0:T(2,128)(2,1)} %shard_map.100) | data formatting | bytes 16384

commit v4 on v3

--- a/solution.py
+++ b/solution.py
@@ -75,6 +75,7 @@
     up_out,
     up_in,
     part,
+    ftile,
     fsend,
     frecv,
     load_sem,
@@ -115,13 +116,13 @@
         pltpu.make_async_copy(src, dst, load_sem.at[n])
         for n, (src, dst) in enumerate(
             (
+                (ckv_hbm, ckvv),
+                (x_hbm, xv),
                 (q_hbm, qbuf.at[z]),
                 (qkv_hbm.at[0], wbuf0.at[me, :, pl.ds(0, HD)]),
                 (qkv_hbm.at[1], wbuf0.at[me, :, pl.ds(HD, HD)]),
                 (qkv_hbm.at[2], wbuf0.at[me, :, pl.ds(2 * HD, HD)]),
                 (ow_hbm, wbuf0.at[me, :, pl.ds(3 * HD, HD)]),
-                (ckv_hbm, ckvv),
-                (x_hbm, xv),
                 (up_hbm, wbuf1.at[z, 0]),
                 (down_hbm, wbuf1.at[z, 1]),
                 (pos_hbm, posv),
@@ -154,8 +155,7 @@
     qx[1] = jnp.zeros((ROWS, HD), BF16)
     rx[...] = jnp.zeros_like(rx)
     greet({"seq": partner})
-    for load in loads[:5]:
-        load.wait()
+    loads[2].wait()
     pl.semaphore_wait(barrier, NZ - 1 + 1 + 2 * (NLAT - 1))
 
     def drain(ref, sem):
@@ -171,7 +171,8 @@
             device_id_type=MESH,
         )
 
-    def send_query(i, carry):
+    def send_query(n, carry):
+        i = 8 + (1 - 2 * lax.rem(n, 2)) * (n // 2)
         remote(qbuf.at[z], qbuf.at[z], qs_sem, qr_sem.at[my_quad], {"seq": in_line(i)}).start()
         return carry
 
@@ -203,15 +204,17 @@
         if 0 < k < 8:
             move(0, lax.rem(z + k, NZ), partner, wx_sem).start()
 
-    ring_start(0)
-
-    loads[5].wait()
-    loads[6].wait()
-    half_rows = TOK // 2
-    for half in range(2):
-        rows = pl.ds(half * half_rows, half_rows)
+    loads[0].wait()
+    loads[1].wait()
+    piece = TOK // 4
+    for n in range(4):
+        rows = pl.ds(n * piece, piece)
         kvt[0, rows, :] = dot_nn(xv[rows, :], ckvv[...]).astype(BF16)
         remote(kvt.at[0, rows], kvt.at[1, rows], xs_sem, xr_sem, {"seq": partner}).start()
+        if n == 0:
+            for load in loads[3:7]:
+                load.wait()
+            ring_start(0)
     for load in loads[7:]:
         load.wait()
     ring_step(0, 1)
@@ -247,7 +250,7 @@
         return carry
 
     def second_pass(j, carry):
-        quad = lax.rem(my_quad + j, 4)
+        quad = lax.rem(my_quad + 1 + j, 4)
         top, total, numer = attend(quad, 1, partner)
         top_1 = part_m[quad]
         best = jnp.maximum(top_1, top)
@@ -278,29 +281,22 @@
     lax.fori_loop(0, 2, first_pass, 0)
     ring_step(0, 2)
     lax.fori_loop(2, 4, first_pass, 0)
+    drain(kvt.at[1], xr_sem)
     ring_step(0, 3)
-    drain(kvt.at[1], xr_sem)
-    for k in range(3):
+    lax.fori_loop(0, 4, second_pass, 0)
+    ring_step(0, 4)
+    ring_start(1)
+    for k in range(5):
         cross(k)
-    lax.fori_loop(0, 2, second_pass, 0)
-    ring_step(0, 4)
-    cross(3)
-    lax.fori_loop(2, 4, second_pass, 0)
-    ring_step(0, 5)
-    cross(4)
-    ring_start(1)
     crecv[z] = csend[z]
     lrecv[z] = lsend[my_quad]
     drain(qbuf.at[pl.ds(0, 15)], qs_sem)
     drain(kvt.at[0], xs_sem)
+    ring_step(0, 5)
+    cross(5)
+    ring_step(1, 1)
     ring_step(0, 6)
-    cross(5)
-    ring_step(0, 7)
     cross(6)
-    ring_step(0, 8)
-    cross(7)
-    cross(8)
-    ring_step(1, 1)
     drain(crecv.at[pl.ds(0, 15)], cr_sem)
     drain(lrecv.at[pl.ds(0, 15)], lr_sem)
 
@@ -351,9 +347,13 @@
 
     my_cols = pl.ds(pl.multiple_of(lme * HD, HD), HD)
     scatter_start(0, dot_nn(context.astype(BF16), wov[...]))
+    ring_step(0, 7)
+    cross(7)
     ring_step(1, 2)
     h = basev[:, my_cols].astype(F32) + scatter_finish(0)
     gather_start(h)
+    ring_step(0, 8)
+    cross(8)
     ring_step(1, 3)
     drain(wbuf0.at[pl.ds(0, 31)], ws_sem.at[0])
     drain(wbuf0.at[pl.ds((1 - xh) * NZ, NZ)], wx_sem)
@@ -380,13 +380,13 @@
 
     drain(crecv.at[pl.ds(0, 15)], cs_sem)
     drain(lrecv.at[pl.ds(0, 15)], ls_sem)
+    ring_step(1, 4)
     kv_move(z + 12, 4, 1).wait_recv()
     for i in range(1, 5):
         kv_move(z + 12, i, 0).start()
     kv_move(z + 4, 12, 2).wait_recv()
     for i in range(13, 16):
         kv_move(z + 4, i, 0).start()
-    ring_step(1, 4)
     ring_step(1, 5)
 
     @pl.when(xh == 0)
@@ -418,20 +418,20 @@
 
     self_ctx = (self_numer[0:ROWS, :] + rx[0:ROWS, :]) / (self_total[0:ROWS, :] + rx[ROWS:, :])
 
-    scatter_start(1, dot_nt(self_ctx.astype(BF16), wbuf0[:, :, 3 * HD :].reshape(D, HD)))
-    ring_step(1, 7)
-    h = h + scatter_finish(1)
-
     home = lme // 8
-    col = lax.rem(lme, 8)
     at_home = xh == home
-    hsend[1] = h.astype(BF16)
-
-    def wide_send(i, carry):
-        @pl.when(jnp.logical_or(i != lme, xh != home))
+    for f in range(NLAT):
+        block = wbuf0[2 * f : 2 * f + 2, :, 3 * HD :].reshape(HD, HD)
+        rsend[1, f] = dot_nt(self_ctx.astype(BF16), block).astype(BF16)
+    rsend[1, lme] = (rsend[1, lme].astype(F32) + h).astype(BF16)
+
+    def wide_send(f, carry):
+        place = xh * 8 + lax.rem(f, 8)
+
+        @pl.when(jnp.logical_or(place != lme, xh != f // 8))
         def _():
-            to = {"seq": home * NZ + z, "lat": i}
-            remote(hsend.at[1], wide_in.at[xh, col], gs_sem.at[1], gr_sem.at[1], to).start()
+            to = {"seq": (f // 8) * NZ + z, "lat": place}
+            remote(rsend.at[1, f], rrecv.at[1, lme], rs_sem.at[1], rr_sem.at[1], to).start()
 
         return carry
 
@@ -448,10 +448,25 @@
 
     @pl.when(at_home)
     def _():
-        wide_in[xh, col] = hsend[1]
-
+        rrecv[1, lme] = rsend[1, lme]
+
+    ring_step(1, 7)
+    wide_wait(rr_sem.at[1])
+    h = rrecv[1, 0].astype(F32)
+    for i in range(1, NLAT):
+        h += rrecv[1, i].astype(F32)
+    hsend[1] = h.astype(BF16)
+    col = lax.rem(lme, 8)
+
+    def second_send(i, carry):
+        to = {"lat": in_lat(i)}
+        remote(hsend.at[1], wide_in.at[home, col], gs_sem.at[1], gr_sem.at[1], to).start()
+        return carry
+
+    lax.fori_loop(1, NLAT, second_send, 0)
+    wide_in[home, col] = hsend[1]
     ring_step(1, 8)
-    wide_wait(gr_sem.at[1])
+    drain(gath.at[pl.ds(0, 15)], gr_sem.at[1])
     rows = jnp.concatenate([wide_in[:, f].reshape(2 * ROWS, HD) for f in range(8)], axis=1)
     wide = rows.astype(F32)
     square = jnp.sum(wide * wide, axis=-1, keepdims=True)
@@ -463,10 +478,10 @@
     half_out = remote(up_out, up_in, ps_sem.at[2], pr_sem.at[2], {"seq": partner})
     half_out.start()
     drain(wbuf1.at[pl.ds(0, 15)], ws_sem.at[1])
-    for n in range(2):
-        drain(rrecv.at[n, pl.ds(1, NLAT - 1)], rs_sem.at[n])
-    drain(gath.at[pl.ds(0, NLAT - 1)], gs_sem.at[0])
-    wide_wait(gs_sem.at[1])
+    drain(gath.at[pl.ds(0, 15)], rs_sem.at[0])
+    wide_wait(rs_sem.at[1])
+    drain(gath.at[pl.ds(0, 15)], gs_sem.at[0])
+    drain(gath.at[pl.ds(0, 15)], gs_sem.at[1])
     drain(kvbuf.at[pl.ds(0, 15)], ks_sem)
     half_out.wait_recv()
     other = up_in[:, HID:].astype(F32)
@@ -475,13 +490,15 @@
     hidden = jax.nn.gelu((up + up_in[:, 0:HID].astype(F32)) * gain).astype(BF16)
     part[...] = dot_nt(hidden, wbuf1[:, 1].reshape(D // 2, HID))
 
-    @pl.when(at_home)
+    @pl.when(lme < 8)
     def _():
         cols = pl.ds(pl.multiple_of(col * HD, HD), HD)
         part[:, cols] += wide_in[:, col].reshape(2 * ROWS, HD).astype(F32)
 
-    for f in range(2 * NLAT):
-        fsend[f] = part[2 * f : 2 * f + 2, :]
+    for p in range(2 * NLAT):
+        for f in range(8):
+            ftile[p, 2 * f : 2 * f + 2, :] = part[2 * p : 2 * p + 2, f * HD : (f + 1) * HD]
+    fsend[...] = ftile[...].astype(BF16)
     mine = xh * NLAT + lme
 
     def last_send(i, carry):
@@ -504,10 +521,12 @@
 
     drain(frecv.at[pl.ds(0, 31)], fr_sem)
     for half in range(2):
-        acc = frecv[half * NLAT]
+        acc = frecv[half * NLAT].astype(F32)
         for i in range(1, NLAT):
-            acc += frecv[half * NLAT + i]
-        out_ref[:, half * (D // 2) : (half + 1) * (D // 2)] = acc.astype(BF16)
+            acc += frecv[half * NLAT + i].astype(F32)
+        for f in range(8):
+            cols = slice(half * (D // 2) + f * HD, half * (D // 2) + (f + 1) * HD)
+            out_ref[:, cols] = acc[2 * f : 2 * f + 2, :].astype(BF16)
     drain(frecv.at[pl.ds(0, 31)], fs_sem)
 
 
@@ -562,8 +581,9 @@
             pltpu.VMEM((2 * ROWS, HID + HD), BF16),
             pltpu.VMEM((2 * ROWS, HID + HD), BF16),
             pltpu.VMEM((2 * ROWS, D // 2), F32),
-            pltpu.VMEM((2 * NLAT, 2, D // 2), F32),
-            pltpu.VMEM((2 * NLAT, 2, D // 2), F32),
+            pltpu.VMEM((2 * NLAT, 16, HD), F32),
+            pltpu.VMEM((2 * NLAT, 16, HD), BF16),
+            pltpu.VMEM((2 * NLAT, 16, HD), BF16),
             dma((12,)),
             dma,
             dma((4,)),

time: 111 us -> 106 us (0.955)
  Pallas kernels: 107 us -> 103 us
    pallas_call x1, Pallas kernels: 107 us -> 103 us  [local(): pl.pallas_call(kernel, out_shape=jax.ShapeDtypeStruct((ROWS // NLAT, D),...]
where the time goes in v4:
time: 106 us
  Pallas kernels  103 us (97%)
  local copies, waits for them, and re-layouts  3.65 us (3%)
    pallas_call x1, Pallas kernels, local(): pl.pallas_call(kernel, out_shape=jax.ShapeDtypeStruct((ROWS // NLAT, D),...  103 us
    unnamed x2, local copies, waits for them, and re-layouts  3.65 us

profile of v4, /device:TPU:1, one launch (start us, length us, event | category | flops | bytes accessed | tf_op | source)
XLA Modules:
  0.0 106.2 jit_solution(8575786198992011103)
XLA Ops:
  0.0 2.4 %copy.13 = bf16[256,8,2,128]{3,1,2,0:T(8,128)(2,1)} copy(bf16[256,8,2,128]{3,2,1,0:T(2,128)(2,1)} %bitcast.12) | data formatting | bytes 2097152
  2.4 102.5 %shard_map.100 = bf16[2,2048]{1,0:T(2,128)(2,1)} custom-call(bf16[768,2048]{1,0:T(8,128)(2,1)} %x_hbm.1, bf16[2048,256]{1,0:T(8,128)(2,1)} %bitcast.11, bf16[128,2048]{1,0:T(8,128)(2,1)} %wo_hbm.1, bf16[32,128]{1,0:T(8,128)(2,1)} %q_hbm.1, bf16[32,2048]{1,0:T(8,128)(2,1)} %base_hbm.1, s32[8,128]{1,0:T(8,128)} %bitcast.17, bf16[3,64,128]{2,1,0:T(8,128)(2,1)} %bitcast.15, ...), custom_call_target="tpu_custom_call" | custom-call | tf_op jit(solution)/shard_map/pallas_call | solution.py:548
  104.9 1.3 %copy.15 = bf16[2,2048]{1,0:T(2,128)(2,1)} copy(bf16[2,2048]{1,0:T(2,128)(2,1)} %shard_map.100) | data formatting | bytes 16384

commit v5 on v4

--- a/solution.py
+++ b/solution.py
@@ -112,12 +112,14 @@
     z_up = line + lax.rem(z + 1, NZ)
     z_down = line + lax.rem(z + NZ - 1, NZ)
 
+    piece = TOK // 4
+    pieces = [pl.ds(n * piece, piece) for n in range(4)]
     loads = [
         pltpu.make_async_copy(src, dst, load_sem.at[n])
         for n, (src, dst) in enumerate(
             (
                 (ckv_hbm, ckvv),
-                (x_hbm, xv),
+                *((x_hbm.at[rows], xv.at[rows]) for rows in pieces),
                 (q_hbm, qbuf.at[z]),
                 (qkv_hbm.at[0], wbuf0.at[me, :, pl.ds(0, HD)]),
                 (qkv_hbm.at[1], wbuf0.at[me, :, pl.ds(HD, HD)]),
@@ -155,7 +157,7 @@
     qx[1] = jnp.zeros((ROWS, HD), BF16)
     rx[...] = jnp.zeros_like(rx)
     greet({"seq": partner})
-    loads[2].wait()
+    loads[5].wait()
     pl.semaphore_wait(barrier, NZ - 1 + 1 + 2 * (NLAT - 1))
 
     def drain(ref, sem):
@@ -205,17 +207,15 @@
             move(0, lax.rem(z + k, NZ), partner, wx_sem).start()
 
     loads[0].wait()
-    loads[1].wait()
-    piece = TOK // 4
-    for n in range(4):
-        rows = pl.ds(n * piece, piece)
+    for n, rows in enumerate(pieces):
+        loads[1 + n].wait()
         kvt[0, rows, :] = dot_nn(xv[rows, :], ckvv[...]).astype(BF16)
         remote(kvt.at[0, rows], kvt.at[1, rows], xs_sem, xr_sem, {"seq": partner}).start()
         if n == 0:
-            for load in loads[3:7]:
+            for load in loads[6:10]:
                 load.wait()
             ring_start(0)
-    for load in loads[7:]:
+    for load in loads[10:]:
         load.wait()
     ring_step(0, 1)
 
@@ -584,7 +584,7 @@
             pltpu.VMEM((2 * NLAT, 16, HD), F32),
             pltpu.VMEM((2 * NLAT, 16, HD), BF16),
             pltpu.VMEM((2 * NLAT, 16, HD), BF16),
-            dma((12,)),
+            dma((15,)),
             dma,
             dma((4,)),
             dma,

time: 106 us -> 106 us (level)
  no operation moved by 1% of the time
where the time goes in v5:
time: 106 us
  Pallas kernels  103 us (97%)
  local copies, waits for them, and re-layouts  3.65 us (3%)
    pallas_call x1, Pallas kernels, local(): pl.pallas_call(kernel, out_shape=jax.ShapeDtypeStruct((ROWS // NLAT, D),...  103 us
    unnamed x2, local copies, waits for them, and re-layouts  3.65 us

profile of v5, /device:TPU:1, one launch (start us, length us, event | category | flops | bytes accessed | tf_op | source)
XLA Modules:
  0.0 106.2 jit_solution(3008966032410054567)
XLA Ops:
  0.0 2.4 %copy.13 = bf16[256,8,2,128]{3,1,2,0:T(8,128)(2,1)} copy(bf16[256,8,2,128]{3,2,1,0:T(2,128)(2,1)} %bitcast.12) | data formatting | bytes 2097152
  2.4 102.6 %shard_map.100 = bf16[2,2048]{1,0:T(2,128)(2,1)} custom-call(bf16[768,2048]{1,0:T(8,128)(2,1)} %x_hbm.1, bf16[2048,256]{1,0:T(8,128)(2,1)} %bitcast.11, bf16[128,2048]{1,0:T(8,128)(2,1)} %wo_hbm.1, bf16[32,128]{1,0:T(8,128)(2,1)} %q_hbm.1, bf16[32,2048]{1,0:T(8,128)(2,1)} %base_hbm.1, s32[8,128]{1,0:T(8,128)} %bitcast.17, bf16[3,64,128]{2,1,0:T(8,128)(2,1)} %bitcast.15, ...), custom_call_target="tpu_custom_call" | custom-call | tf_op jit(solution)/shard_map/pallas_call | solution.py:548
  104.9 1.3 %copy.15 = bf16[2,2048]{1,0:T(2,128)(2,1)} copy(bf16[2,2048]{1,0:T(2,128)(2,1)} %shard_map.100) | data formatting | bytes 16384
